TPU v7x, 512 devices: a whole 4x4x16 slice. The times are simulated.
512 devices in a mesh: leaf: 64 (over y, z), cols: 8 (over x, core).
Axes of the slice: x: 4, y: 4, z: 16, core: 2. Of those that a mesh axis runs over, the one named last changes fastest.
Arguments:
- points: float32 [3, 131072], P(None, 'leaf'), may hold values from 0 to 1
- samples: float32 [256, 131072], P('cols', 'leaf'), may hold values from -6 to 6
- sketch: float32 [32, 256], P(None, 'cols'), may hold values from -0.375 to 0.375
- far_requests: int32 [64, 64, 8], P('leaf'), may hold values from 0 to 31, as said below
- far_slots: int32 [2048, 16], P('leaf'), may hold values from 0 to 511, as said below
- far_count: int32 [2048], P('leaf'), may hold values from 1 to 16, as said below
- near_mask: int32 [2048, 3], P('leaf'), may hold values 0 or 1
Outputs:
- far_sample: float32 [256, 131072], P('cols', 'leaf')
- near_sample: float32 [256, 131072], P('cols', 'leaf')
- leaf_basis: float32 [32, 131072], P(None, 'leaf')
- branch_samples: float32 [2048, 256], P('leaf', 'cols')
- top_transfer: float32 [63, 64, 32], replicated
- root_sample: float32 [32, 256], P(None, 'cols')
Inputs may be any that keep to these rules, and one draw needn't show every extreme that they name: far_requests[e, d, c] is a leaf counted on device d of leaf (0 for its first); the 8 entries of each [e, d] are distinct. far_slots[i, f] names slot far_slots[i, f] mod 8 of the clusters fetched from device far_slots[i, f] // 8; only entries f < far_count[i] are used; among the 512 entries (used or not) of the leaves of one device, no device is named by more than 8 entries, and some device by exactly 8. `far_count`: used entries of each leaf's far-field list.
All inputs are finite; a program needn't handle non-finite values. No bound on the sum of `near_mask` on one device may be relied on, other than what follows from the above.
Results may differ from a plain program's by a relative error of at most 0.0003.
Values sent between devices are 32-bit elements; how exact they have to be, the bound alone decides.
A program may use at most 64 MiB of HBM per device.

v0:
```python
import functools

import jax
import jax.numpy as jnp
from jax import lax
from jax.experimental import pallas as pl
from jax.experimental.pallas import tpu as pltpu
from jax.sharding import PartitionSpec as P

LEAF = 64
FAR = 16
CAP = 8
RANK = 32
NEAR = 3
ROWS_Y = 4
CELL = 16
HALF = 16
SUB = HALF * CELL + HALF * 2
MSG = CAP * CELL + CAP * 2
NODE = 24

length_scale = 0.3
shift_share = 0.05
highest = lax.Precision.HIGHEST
MESH = pl.DeviceIdType.MESH
VMEM = pltpu.VMEM
whole = pl.BlockSpec(memory_space=pltpu.VMEM)
scalars = pl.BlockSpec(memory_space=pltpu.SMEM)
MIB = 1 << 20


def lanes(shape):
    return lax.broadcasted_iota(jnp.int32, shape, len(shape) - 1)


def swap_halves(tile):
    return pltpu.roll(tile, 64, 1)


def dot_nt(a, b, precision=highest):
    return lax.dot_general(
        a, b, (((1,), (1,)), ((), ())), precision=precision, preferred_element_type=jnp.float32
    )


def dot_nn(a, b, precision=highest):
    return lax.dot_general(
        a, b, (((1,), (0,)), ((), ())), precision=precision, preferred_element_type=jnp.float32
    )


def greet(axis, peers):
    barrier = pltpu.get_barrier_semaphore()
    for peer in peers:
        pl.semaphore_signal(barrier, inc=1, device_id={axis: peer}, device_id_type=MESH)
    pl.semaphore_wait(barrier, len(peers))


def fetch_body(
    n_leaf, samples, points, sent_requests, recv, local, halo, *scratch
):
    n_y = ROWS_Y
    n_z = n_leaf // n_y
    chunks = (local,) + scratch[: n_z - 1]
    stage, edge, asked_v, asked, ring_send, ring_recv, y_send, y_recv, q_send, q_recv, q_local, e_send, e_recv = scratch[n_z - 1 :]
    me = lax.axis_index("leaf")
    y, z = me // n_z, me % n_z
    up = y * n_z + (z + 1) % n_z
    down = y * n_z + (z + n_z - 1) % n_z
    above, below = (me + 1) % n_leaf, (me + n_leaf - 1) % n_leaf
    across = [None] + [((y + k) % n_y) * n_z + z for k in range(1, n_y)]
    greet("leaf", [up, down, above, below] + across[1:])

    def remote(src, dst, send, recv_sem, peer):
        return pltpu.make_async_remote_copy(
            src_ref=src, dst_ref=dst, send_sem=send, recv_sem=recv_sem,
            device_id={"leaf": peer}, device_id_type=MESH,
        )

    sent = []
    asks = []
    for k in range(1, n_y):
        copy = remote(
            sent_requests.at[(y + k) % n_y], asked_v.at[n_y - k - 1], q_send.at[k - 1], q_recv.at[n_y - k - 1], across[k]
        )
        copy.start()
        asks.append(copy)
    sent += asks

    low = lanes((CELL, 2 * LEAF)) < LEAF
    for j in range(HALF):
        top = samples[0:CELL, 2 * LEAF * j : 2 * LEAF * (j + 1)]
        bottom = samples[CELL : 2 * CELL, 2 * LEAF * j : 2 * LEAF * (j + 1)]
        base = (2 * j // HALF) * SUB + (2 * j % HALF) * CELL
        local[base : base + CELL, :] = jnp.where(low, top, swap_halves(bottom))
        local[base + CELL : base + 2 * CELL, :] = jnp.where(low, swap_halves(top), bottom)
    low1 = lanes((1, 2 * LEAF)) < LEAF
    for j in range(HALF):
        xs, ys, zs = [points[a : a + 1, 2 * LEAF * j : 2 * LEAF * (j + 1)] for a in range(3)]
        base = (2 * j // HALF) * SUB + HALF * CELL + (2 * j % HALF) * 2
        local[base : base + 1, :] = jnp.where(low1, xs, swap_halves(ys))
        local[base + 1 : base + 2, :] = jnp.where(low1, zs, swap_halves(zs))
        local[base + 2 : base + 3, :] = jnp.where(low1, swap_halves(xs), ys)
        local[base + 3 : base + 4, :] = jnp.where(low1, swap_halves(zs), zs)

    hops = {(0, 0): n_z // 2, (0, 1): n_z // 2 - 1, (1, 0): n_z // 2 - 1, (1, 1): n_z // 2}

    def ring(way, part, step):
        here, there = (step, step + 1) if way == 0 else ((n_z - step) % n_z, n_z - step - 1)
        rows = pl.ds(part * SUB, SUB)
        return remote(
            chunks[here].at[rows], chunks[there].at[rows], ring_send.at[way, part, step],
            ring_recv.at[way, part, step], up if way == 0 else down,
        )

    def forward(way, part, step):
        if step < hops[way, part]:
            copy = ring(way, part, step)
            copy.start()
            sent.append(copy)

    order = ((0, 0), (1, 1), (0, 1), (1, 0))
    for way, part in order:
        forward(way, part, 0)

    for side, cluster in ((0, 0), (1, 2 * HALF - 1)):
        base = (cluster // HALF) * SUB + (cluster % HALF) * CELL
        cbase = (cluster // HALF) * SUB + HALF * CELL + (cluster % HALF) * 2
        edge[side, 0:CELL, :] = local[base : base + CELL, :]
        edge[side, CELL : CELL + 2, :] = local[cbase : cbase + 2, :]
        edge[side, CELL + 2 : NODE, :] = jnp.zeros((NODE - CELL - 2, 2 * LEAF), jnp.float32)
    edges = [
        remote(edge.at[0], halo.at[1], e_send.at[0], e_recv.at[1], below),
        remote(edge.at[1], halo.at[0], e_send.at[1], e_recv.at[0], above),
    ]
    for copy in edges:
        copy.start()
    sent += edges

    for copy in asks:
        copy.wait_recv()
    moves = [
        pltpu.make_async_copy(asked_v, asked.at[pl.ds(1, n_y - 1)], q_local.at[0]),
        pltpu.make_async_copy(sent_requests.at[y], asked.at[0], q_local.at[1]),
    ]
    for move in moves:
        move.start()
    for move in moves:
        move.wait()

    def pick(chunk, target, request):
        def one(c, carry):
            cell, row = request(c)
            target[pl.ds(pl.multiple_of(c * CELL, CELL), CELL), :] = chunk[pl.ds(cell * CELL, CELL), :]
            for part in range(2):
                target[pl.ds(CAP * CELL + c * 2 + part, 1), :] = chunk[pl.ds(row + part, 1), :]
            return carry

        lax.fori_loop(0, CAP, one, 0)

    arriving = []

    def select(slot):
        chunk = chunks[slot]
        source_z = (z + n_z - slot) % n_z

        def requests(k):
            return lambda c: (asked[k, 0, source_z * CAP + c], asked[k, 1, source_z * CAP + c])

        for k in range(1, n_y):
            pick(chunk, stage.at[k - 1, slot], requests(k))
            copy = remote(
                stage.at[k - 1, slot], recv.at[k * n_z + slot], y_send.at[k - 1, slot], y_recv.at[k - 1, slot], across[k]
            )
            copy.start()
            sent.append(copy)
            arriving.append(copy)
        pick(chunk, recv.at[slot], requests(0))

    select(0)
    for step in range(1, n_z // 2 + 1):
        for way, part in order:
            if step - 1 < hops[way, part]:
                ring(way, part, step - 1).wait_recv()
                forward(way, part, step)
        select(step)
        if step < n_z // 2:
            select(n_z - step)
    for copy in arriving + edges:
        copy.wait_recv()
    for copy in sent:
        copy.wait_send()


def fetch(samples, points, requests, n_leaf):
    n_z = n_leaf // ROWS_Y
    rows = samples.shape[0]
    half, cell = requests // HALF, requests % HALF
    places = jnp.stack([half * (SUB // CELL) + cell, half * SUB + HALF * CELL + cell * 2])
    sent_requests = jnp.swapaxes(places.reshape(2, ROWS_Y, n_z * CAP), 0, 1)
    sent_requests = jnp.pad(sent_requests, ((0, 0), (0, 6), (0, 0)))
    dma = pltpu.SemaphoreType.DMA
    f32 = jnp.float32
    return pl.pallas_call(
        functools.partial(fetch_body, n_leaf),
        out_shape=(
            jax.ShapeDtypeStruct((n_leaf, MSG, 2 * LEAF), f32),
            jax.ShapeDtypeStruct((2 * SUB, 2 * LEAF), f32),
            jax.ShapeDtypeStruct((2, NODE, 2 * LEAF), f32),
        ),
        in_specs=[whole, whole, whole],
        out_specs=(whole, whole, whole),
        scratch_shapes=[VMEM((2 * SUB, 2 * LEAF), f32)] * (n_z - 1)
        + [
            VMEM((ROWS_Y - 1, n_z, MSG, 2 * LEAF), f32),
            VMEM((2, NODE, 2 * LEAF), f32),
            VMEM((ROWS_Y - 1, 8, n_z * CAP), jnp.int32),
            pltpu.SMEM((ROWS_Y, 8, n_z * CAP), jnp.int32),
            dma((2, 2, n_z // 2)),
            dma((2, 2, n_z // 2)),
            dma((ROWS_Y - 1, n_z)),
            dma((ROWS_Y - 1, n_z)),
            dma((ROWS_Y - 1,)),
            dma((ROWS_Y - 1,)),
            dma((2,)),
            dma((2,)),
            dma((2,)),
        ],
        compiler_params=pltpu.CompilerParams(
            collective_id=1, has_side_effects=True, vmem_limit_bytes=40 * MIB
        ),
        name="fetch",
    )(samples, points, sent_requests)


def sample_body(
    leaves, n_leaf, recv, local, halo, points, slots, counts, near, sketch, far_out, near_out, partial_out, cells
):
    n_z = n_leaf // ROWS_Y
    me = lax.axis_index("leaf")
    y, z = me // n_z, me % n_z
    low16 = lanes((CELL, 2 * LEAF)) < LEAF
    low1 = lanes((1, 2 * LEAF)) < LEAF
    low32 = lanes((2 * CELL, 2 * LEAF)) < LEAF
    for c in range(leaves):
        base = (c // HALF) * SUB + (c % HALF) * CELL
        cbase = (c // HALF) * SUB + HALF * CELL + (c % HALF) * 2
        cells[c + 1, 0:CELL, :] = local[base : base + CELL, :]
        cells[c + 1, CELL : CELL + 2, :] = local[cbase : cbase + 2, :]
    cells[0] = halo[0]
    cells[leaves + 1] = halo[1]

    def halves(value):
        high = value.astype(jnp.bfloat16)
        return high, (value - high.astype(jnp.float32)).astype(jnp.bfloat16)

    def pair(coordinates, first, second):
        (block_a, row_a, last_a, scale_a), (block_b, row_b, last_b, scale_b) = first, second
        x = jnp.where(low1, row_a, swap_halves(row_b))
        yy = jnp.where(low1, swap_halves(row_a), row_b)
        zz = jnp.where(low1, last_a, last_b)
        dx = coordinates[0] - x
        dy = coordinates[1] - yy
        dz = coordinates[2] - zz
        square = dx * dx + dy * dy + dz * dz
        values = jnp.exp2(square * lax.rsqrt(jnp.maximum(square, 1e-30)) * (-1.4426950408889634 / length_scale))
        block_a = block_a * scale_a
        block_b = block_b * scale_b
        rows = jnp.concatenate(
            [jnp.where(low16, block_a, swap_halves(block_b)), jnp.where(low16, swap_halves(block_a), block_b)], axis=0
        )
        return halves(values), halves(rows)

    def four(coordinates, entries):
        (k0h, k0l), (s0h, s0l) = pair(coordinates, entries[0], entries[1])
        (k1h, k1l), (s1h, s1l) = pair(coordinates, entries[2], entries[3])
        left = jnp.concatenate(
            [jnp.concatenate([s0h, s1h], axis=1), jnp.concatenate([s0l, s1l], axis=1)], axis=0
        )
        right = jnp.concatenate(
            [jnp.concatenate([k0h, k1h], axis=1), jnp.concatenate([k0l, k1l], axis=1)], axis=0
        )
        return left, right

    def far_entry(leaf, f, count):
        slot = slots[f, leaf]
        owner = slot >> 3
        message = ((y - owner // n_z) & (ROWS_Y - 1)) * n_z + ((z - owner) & (n_z - 1))
        c = slot & (CAP - 1)
        scale = jnp.where(f < count, 1.0, 0.0).astype(jnp.float32)
        return (
            recv[message, pl.ds(pl.multiple_of(c * CELL, CELL), CELL), :],
            recv[message, pl.ds(CAP * CELL + 2 * c, 1), :],
            recv[message, pl.ds(CAP * CELL + 2 * c + 1, 1), :],
            scale,
        )

    def near_entry(leaf, offset):
        at = leaf + offset
        if offset < NEAR:
            place = me * leaves + leaf + offset - NEAR // 2
            inside = (place >= 0) & (place < n_leaf * leaves)
            scale = jnp.where(inside, near[offset, leaf], 0).astype(jnp.float32)
        else:
            scale = jnp.float32(0)
        at = at if offset < NEAR else leaf
        return cells[at, 0:CELL, :], cells[at, CELL : CELL + 1, :], cells[at, CELL + 1 : CELL + 2, :], scale

    def fold(total):
        total = total[: 2 * CELL] + total[2 * CELL :]
        return total + swap_halves(total)

    def two_leaves(j, carry):
        pair_of = (2 * j, 2 * j + 1)
        coordinates = []
        both = points[:, pl.ds(pl.multiple_of(j * 2 * LEAF, 2 * LEAF), 2 * LEAF)]
        both = jnp.concatenate([both, jnp.zeros((5, 2 * LEAF), jnp.float32)], axis=0).T
        for block in (both[:LEAF], both[LEAF:]):
            coordinates.append([jnp.broadcast_to(block[:, a : a + 1], (LEAF, 2 * LEAF)) for a in range(3)])
        count = [counts[leaf] for leaf in pair_of]

        def operands(g):
            return [
                four(coordinates[i], [far_entry(pair_of[i], 4 * g + b, count[i]) for b in range(4)]) for i in range(2)
            ]

        def step(g, carried):
            totals, waiting = carried
            totals = [total + dot_nt(left, right, None) for total, (left, right) in zip(totals, waiting)]
            return totals, operands(g)

        zero = jnp.zeros((LEAF, 2 * LEAF), jnp.float32)
        steps = (jnp.maximum(count[0], count[1]) + 3) // 4
        totals, waiting = lax.fori_loop(1, steps, step, ([zero, zero], operands(0)))
        far = [total + dot_nt(left, right, None) for total, (left, right) in zip(totals, waiting)]
        close = [four(coordinates[i], [near_entry(pair_of[i], o) for o in range(4)]) for i in range(2)]
        close = [dot_nt(left, right, None) for left, right in close]
        far = jnp.where(low32, fold(far[0]), fold(far[1]))
        at = pl.ds(pl.multiple_of(j * 2 * LEAF, 2 * LEAF), 2 * LEAF)
        far_out[:, at] = far
        near_out[:, at] = jnp.where(low32, fold(close[0]), fold(close[1]))
        partial_out[:, at] = dot_nn(sketch[...], far)
        return carry

    lax.fori_loop(0, leaves // 2, two_leaves, 0)


def sample(recv, local, halo, points, slots, counts, near, sketch, n_leaf):
    leaves = counts.shape[0]
    shape = jax.ShapeDtypeStruct((RANK, leaves * LEAF), jnp.float32)
    return pl.pallas_call(
        functools.partial(sample_body, leaves, n_leaf),
        out_shape=(shape, shape, shape),
        in_specs=[whole, whole, whole, whole, scalars, scalars, scalars, whole],
        out_specs=(whole, whole, whole),
        scratch_shapes=[VMEM((leaves + 2, NODE, 2 * LEAF), jnp.float32)],
        compiler_params=pltpu.CompilerParams(vmem_limit_bytes=40 * MIB),
        name="sample",
    )(recv, local, halo, points, slots, counts, near, sketch)


def total_body(n, partial, out, parts, send_a, recv_a, send_b, recv_b):
    me = lax.axis_index("cols")
    width = partial.shape[1] // n
    peers = [(me + k) % n for k in range(1, n)]
    greet("cols", peers)

    def piece(owner):
        return pl.ds(pl.multiple_of(owner * width, width), width)

    first = []
    for k in range(1, n):
        copy = pltpu.make_async_remote_copy(
            src_ref=partial.at[:, piece(peers[k - 1])], dst_ref=parts.at[k - 1], send_sem=send_a.at[k - 1],
            recv_sem=recv_a.at[k - 1], device_id={"cols": peers[k - 1]}, device_id_type=MESH,
        )
        copy.start()
        first.append(copy)
    value = partial[:, piece(me)]
    for k in range(1, n):
        first[k - 1].wait_recv()
        value = value + parts[k - 1]
    out[:, piece(me)] = value
    second = []
    for k in range(1, n):
        copy = pltpu.make_async_remote_copy(
            src_ref=out.at[:, piece(me)], dst_ref=out.at[:, piece(me)], send_sem=send_b.at[k - 1],
            recv_sem=recv_b.at[k - 1], device_id={"cols": peers[k - 1]}, device_id_type=MESH,
        )
        copy.start()
        second.append(copy)
    for k in range(1, n):
        owner = (me + n - k) % n
        pltpu.make_async_remote_copy(
            src_ref=out.at[:, piece(owner)], dst_ref=out.at[:, piece(owner)], send_sem=send_b.at[k - 1],
            recv_sem=recv_b.at[k - 1], device_id={"cols": peers[k - 1]}, device_id_type=MESH,
        ).wait_recv()
    for copy in first + second:
        copy.wait_send()


def total(partial, n):
    rows, columns = partial.shape
    dma = pltpu.SemaphoreType.DMA
    return pl.pallas_call(
        functools.partial(total_body, n),
        out_shape=jax.ShapeDtypeStruct(partial.shape, jnp.float32),
        in_specs=[whole],
        out_specs=whole,
        scratch_shapes=[VMEM((n - 1, rows, columns // n), jnp.float32)] + [dma((n - 1,))] * 4,
        compiler_params=pltpu.CompilerParams(collective_id=2, has_side_effects=True),
        name="total",
    )(partial)


def eye(shape, first=0):
    rows = lax.broadcasted_iota(jnp.int32, shape, 0)
    return jnp.where(lanes(shape) == rows + first, 1.0, 0.0).astype(jnp.float32)


def inverse(value):
    guess = pl.reciprocal(value, approx=True)
    guess = guess * (2.0 - value * guess)
    return guess * (2.0 - value * guess)


def compress(tiles, traces):
    block = 4 if len(tiles) > 8 else 8
    shape = (RANK, 4 * RANK)
    on_diagonal = lanes(shape) == lax.broadcasted_iota(jnp.int32, shape, 0)
    tiles = [
        tile + jnp.where(on_diagonal, shift_share * trace / RANK + 1e-06, 0.0) for tile, trace in zip(tiles, traces)
    ]
    tiles = [[tile[8 * g : 8 * g + 8] for g in range(4)] for tile in tiles]
    full = (8, 4 * RANK)
    sub = lax.broadcasted_iota(jnp.int32, full, 0)
    scales = [[jnp.zeros(full, jnp.float32) for g in range(4)] for tile in tiles]
    for first in range(0, RANK, block):
        g = first // 8
        columns = [
            [[jnp.broadcast_to(part[:, first + t : first + t + 1], full) for t in range(block)] for part in tile[g:]]
            for tile in tiles
        ]
        for t in range(block):
            s = (first + t) % 8
            for tile, column, scale in zip(tiles, columns, scales):
                pivot = jnp.broadcast_to(column[0][t][s : s + 1], full)
                inv = inverse(pivot)
                scale[g] = jnp.where(sub == s, lax.rsqrt(pivot), scale[g])
                row = jnp.broadcast_to(tile[g][s : s + 1], full) * inv
                right = [None] * block
                for u in range(t + 1, block):
                    right[u] = jnp.broadcast_to(column[0][u][s : s + 1], full) * inv
                for h in range(g, 4):
                    c = column[h - g][t]
                    if h == g:
                        if s == 7:
                            continue
                        c = jnp.where(sub > s, c, 0.0)
                    tile[h] = tile[h] - c * row
                    for u in range(t + 1, block):
                        column[h - g][u] = column[h - g][u] - c * right[u]
    return [
        jnp.concatenate([part * factor for part, factor in zip(tile, scale)], axis=0)
        for tile, scale in zip(tiles, scales)
    ]


def halves(value):
    high = value.astype(jnp.bfloat16)
    return high, (value - high.astype(jnp.float32)).astype(jnp.bfloat16)


def total_of(value):
    return jnp.sum(jnp.sum(value, axis=0, keepdims=True), axis=1, keepdims=True)


def parent_tile(stacked):
    lane = lanes(stacked.shape)
    c = jnp.where(lane < RANK, stacked, 0.0)
    right = jnp.where(lane < 2 * RANK, c + pltpu.roll(c, RANK, 1), eye(stacked.shape, 2 * RANK))
    tile = lax.dot_general(
        c[:, :RANK], right, (((0,), (0,)), ((), ())), precision=highest, preferred_element_type=jnp.float32
    )
    return tile, total_of(c * c)


def project(tile, stacked):
    low = lanes(tile.shape) < 2 * RANK
    high, rest = halves(tile)
    s_high, s_rest = halves(stacked)
    high = high.astype(jnp.float32)
    first = jnp.where(low, swap_halves(rest.astype(jnp.float32)), high)
    left = jnp.concatenate([first, swap_halves(high)], axis=1)[:, : 6 * RANK].astype(jnp.bfloat16)
    return dot_nn(left, jnp.concatenate([s_high, s_high, s_rest], axis=0), None)


def level(read, write, count, group):
    def some(start):
        inputs = [read(start + b) for b in range(min(group, count))]
        pairs = [parent_tile(c) for c, _ in inputs]
        tiles = compress([tile for tile, _ in pairs], [trace for _, trace in pairs])
        for b, (tile, (_, stacked)) in enumerate(zip(tiles, inputs)):
            write(start + b, tile, project(tile, stacked))

    if count <= group:
        some(0)
    else:
        lax.fori_loop(0, count // group, lambda g, carry: (some(g * group), carry)[1], 0)


def branch_body(leaves, sketched, far, basis, branch, packed_c, packed_p, nodes, projected):
    low = lanes((RANK, 2 * LEAF)) < LEAF
    unit = eye((2 * RANK, 2 * RANK))
    group = 16

    def project_t(tile, row):
        high, rest = [part.astype(jnp.float32) for part in halves(tile)]
        r_high, r_rest = [part.astype(jnp.float32) for part in halves(row)]
        left = [jnp.where(low, swap_halves(rest), high), jnp.where(low, 0.0, high)]
        right = [jnp.where(low, swap_halves(r_high), r_high), r_rest]
        return dot_nt(
            jnp.concatenate(left, axis=1).astype(jnp.bfloat16), jnp.concatenate(right, axis=1).astype(jnp.bfloat16), None
        )

    def some(g, carry):
        bs, rows = [], []
        for j in range(group // 2):
            at = pl.ds(pl.multiple_of((g * (group // 2) + j) * 2 * LEAF, 2 * LEAF), 2 * LEAF)
            b, row = sketched[:, at], far[:, at]
            bs += [b[:, :LEAF], swap_halves(b)[:, :LEAF]]
            rows += [swap_halves(row), row]
        tiles = compress([dot_nt(b, jnp.concatenate([b, b, unit], axis=0)) for b in bs], [total_of(b * b) for b in bs])
        for b, (tile, row) in enumerate(zip(tiles, rows)):
            nodes[g * group + b] = tile
            projected[g * group + b] = project_t(tile, row)
        for j in range(group // 2):
            at = pl.ds(pl.multiple_of((g * (group // 2) + j) * 2 * LEAF, 2 * LEAF), 2 * LEAF)
            basis[:, at] = jnp.where(low, swap_halves(tiles[2 * j]), tiles[2 * j + 1])
        return carry

    lax.fori_loop(0, leaves // group, some, 0)

    def read(node):
        pair = nodes[pl.ds(2 * node, 2)].reshape(2 * RANK, 4 * RANK)
        return pltpu.roll(pair, 3 * RANK, 1), projected[pl.ds(2 * node, 2)].reshape(2 * RANK, RANK)

    def write(node, tile, value):
        nodes[node] = tile
        projected[node] = value

    count = leaves // 2
    while count >= 1:
        level(read, write, count, 16)
        count //= 2
    branch[...] = projected[0]
    quarter = lanes((8, 4 * RANK)) // RANK
    wide = dot_nn(projected[0], eye((RANK, 4 * RANK)))
    tile = nodes[0]
    for i, (source, shift) in enumerate(((tile, RANK), (wide, 0))):
        row = jnp.zeros((8, 4 * RANK), jnp.float32)
        for g in range(4):
            turned = pltpu.roll(source[8 * g : 8 * g + 8], (RANK * g - shift) % (4 * RANK), 1)
            row = jnp.where(quarter == g, turned, row)
        if i == 0:
            for g in range(8):
                packed_c[g] = row[g : g + 1]
        else:
            packed_p[...] = row


def meet(n_leaf, n_cols):
    n_y = ROWS_Y
    n_z = n_leaf // n_y
    me, col = lax.axis_index("leaf"), lax.axis_index("cols")
    y, z = me // n_z, me % n_z
    across = [((y + k) % n_y) * n_z + z for k in range(1, n_y)]
    along = [y * n_z + (z + k) % n_z for k in range(1, n_z)]
    others = [(col + k) % n_cols for k in range(1, n_cols)]
    barrier = pltpu.get_barrier_semaphore()
    for peer in across + along:
        pl.semaphore_signal(barrier, inc=1, device_id={"leaf": peer}, device_id_type=MESH)
    for peer in others:
        pl.semaphore_signal(barrier, inc=1, device_id={"cols": peer}, device_id_type=MESH)
    return lambda: pl.semaphore_wait(barrier, len(across) + len(along) + len(others))


def gather_body(n_leaf, n_cols, packed_c, packed_p, out_c, out_p, sems):
    yc_send, yc_recv, yp_send, yp_recv, zc_send, zc_recv, zp_send, zp_recv, x_send, x_recv, own = sems
    n_y = ROWS_Y
    n_z = n_leaf // n_y
    me, col = lax.axis_index("leaf"), lax.axis_index("cols")
    y, z = me // n_z, me % n_z
    across = [((y + k) % n_y) * n_z + z for k in range(1, n_y)]
    along = [y * n_z + (z + k) % n_z for k in range(1, n_z)]
    others = [(col + k) % n_cols for k in range(1, n_cols)]
    sent = []

    def push(src, dst, send, recv, axis, peer):
        copy = pltpu.make_async_remote_copy(
            src_ref=src, dst_ref=dst, send_sem=send, recv_sem=recv, device_id={axis: peer}, device_id_type=MESH
        )
        copy.start()
        sent.append(copy)

    def arrived(ref, send, recv, axis, peer):
        pltpu.make_async_remote_copy(
            src_ref=ref, dst_ref=ref, send_sem=send, recv_sem=recv, device_id={axis: peer}, device_id_type=MESH
        ).wait_recv()

    for k in range(n_y - 1):
        push(packed_c.at[col], out_c.at[col, z, y], yc_send.at[k], yc_recv.at[k], "leaf", across[k])
    for k in range(n_y - 1):
        push(packed_p, out_p.at[z, y], yp_send.at[k], yp_recv.at[k], "leaf", across[k])
    mine = [
        pltpu.make_async_copy(packed_c.at[col], out_c.at[col, z, y], own.at[0]),
        pltpu.make_async_copy(packed_p, out_p.at[z, y], own.at[1]),
    ]
    for copy in mine:
        copy.start()
    for copy in mine:
        copy.wait()
    far_first = sorted(range(n_z - 1), key=lambda k: -min(k + 1, n_z - 1 - k))
    for k in range(n_y - 1):
        arrived(out_c.at[col, z, (y + n_y - k - 1) % n_y], yc_send.at[k], yc_recv.at[k], "leaf", across[k])
    for k in far_first:
        push(out_c.at[col, z], out_c.at[col, z], zc_send.at[k], zc_recv.at[k], "leaf", along[k])
    for k in range(n_y - 1):
        arrived(out_p.at[z, (y + n_y - k - 1) % n_y], yp_send.at[k], yp_recv.at[k], "leaf", across[k])
    for k in far_first:
        push(out_p.at[z], out_p.at[z], zp_send.at[k], zp_recv.at[k], "leaf", along[k])
    for k in range(n_z - 1):
        arrived(out_c.at[col, (z + n_z - k - 1) % n_z], zc_send.at[k], zc_recv.at[k], "leaf", along[k])
    for k in range(n_cols - 1):
        push(out_c.at[col], out_c.at[col], x_send.at[k], x_recv.at[k], "cols", others[k])
    for k in range(n_cols - 1):
        arrived(out_c.at[(col + n_cols - k - 1) % n_cols], x_send.at[k], x_recv.at[k], "cols", others[k])

    def later():
        for k in range(n_z - 1):
            arrived(out_p.at[(z + n_z - k - 1) % n_z], zp_send.at[k], zp_recv.at[k], "leaf", along[k])

    def end():
        for copy in sent:
            copy.wait_send()

    return later, end


def top_body(n_leaf, gathered_c, gathered_p, transfers, root, nodes, projected, later):
    n_z = n_leaf // ROWS_Y
    count = n_leaf // 2

    def unpack(block):
        return jnp.concatenate([pltpu.roll(block, (4 * RANK - RANK * g) % (4 * RANK), 1) for g in range(4)], axis=0)

    def children(node):
        return [(child % n_z, child // n_z) for child in (2 * node, 2 * node + 1)]

    def first_level(g, carry):
        stacked = []
        for b in range(16):
            pair = children(16 * g + b)
            stacked.append(
                jnp.concatenate(
                    [unpack(jnp.concatenate([gathered_c[i, z, y] for i in range(8)], axis=0)) for z, y in pair], axis=0
                )
            )
        pairs = [parent_tile(c) for c in stacked]
        tiles = compress([tile for tile, _ in pairs], [trace for _, trace in pairs])
        for b in range(16):
            nodes[16 * g + b] = tiles[b]
            transfers[16 * g + b] = swap_halves(tiles[b])[:, : 2 * RANK]
        return carry

    lax.fori_loop(0, count // 16, first_level, 0)
    later()

    def first_projections(g, carry):
        for b in range(16):
            node = 16 * g + b
            stacked = jnp.concatenate([unpack(gathered_p[z, y]) for z, y in children(node)], axis=0)
            projected[node] = project(nodes[node], stacked)
        return carry

    lax.fori_loop(0, count // 16, first_projections, 0)

    def read(node):
        pair = nodes[pl.ds(2 * node, 2)].reshape(2 * RANK, 4 * RANK)
        return pltpu.roll(pair, 3 * RANK, 1), projected[pl.ds(2 * node, 2)].reshape(2 * RANK, 4 * RANK)

    first = count
    count //= 2
    while count >= 1:

        def write(node, tile, value, first=first):
            nodes[node] = tile
            projected[node] = value
            transfers[first + node] = swap_halves(tile)[:, : 2 * RANK]

        level(read, write, count, 16)
        first += count
        count //= 2
    root[...] = projected[0][:, :RANK]


def tree_body(
    leaves, n_leaf, n_cols, sketched, far, basis, branch, transfers, root,
    nodes, projected, upper, packed_c, packed_p, out_c, out_p, *sems,
):
    wait = meet(n_leaf, n_cols)
    branch_body(leaves, sketched, far, basis, branch, packed_c, packed_p, nodes, projected)
    wait()
    later, end = gather_body(n_leaf, n_cols, packed_c, packed_p, out_c, out_p, sems)
    top_body(n_leaf, out_c, out_p, transfers, root, nodes, upper, later)
    end()


def tree(sketched, far, n_leaf, n_cols):
    leaves = sketched.shape[1] // LEAF
    n_z = n_leaf // ROWS_Y
    f32 = jnp.float32
    dma = pltpu.SemaphoreType.DMA
    count = max(leaves, n_leaf // 2)
    return pl.pallas_call(
        functools.partial(tree_body, leaves, n_leaf, n_cols),
        out_shape=(
            jax.ShapeDtypeStruct(sketched.shape, f32),
            jax.ShapeDtypeStruct((RANK, RANK), f32),
            jax.ShapeDtypeStruct((n_leaf - 1, RANK, 2 * RANK), f32),
            jax.ShapeDtypeStruct((RANK, RANK), f32),
        ),
        in_specs=[whole, whole],
        out_specs=(whole, whole, whole, whole),
        scratch_shapes=[
            VMEM((count, RANK, 4 * RANK), f32),
            VMEM((leaves, RANK, RANK), f32),
            VMEM((n_leaf // 2, RANK, 4 * RANK), f32),
            VMEM((8, 1, 4 * RANK), f32),
            VMEM((8, 4 * RANK), f32),
            VMEM((8, n_z, ROWS_Y, 1, 4 * RANK), f32),
            VMEM((n_z, ROWS_Y, 8, 4 * RANK), f32),
        ]
        + [dma((ROWS_Y - 1,))] * 4
        + [dma((n_z - 1,))] * 4
        + [dma((n_cols - 1,))] * 2
        + [dma((2,))],
        compiler_params=pltpu.CompilerParams(
            collective_id=3, has_side_effects=True, vmem_limit_bytes=40 * MIB
        ),
        name="tree",
    )(sketched, far)


def on_device(n_leaf, n_cols, points, samples, sketch, far_requests, far_slots, far_count, near_mask):
    recv, local, halo = fetch(samples, points, far_requests[0], n_leaf)
    far_sample, near_sample, partial = sample(
        recv, local, halo, points, far_slots.T, far_count, near_mask.T, sketch, n_leaf
    )
    sketched = total(partial, n_cols)
    leaf_basis, branch_samples, top_transfer, root_sample = tree(sketched, far_sample, n_leaf, n_cols)
    return far_sample, near_sample, leaf_basis, branch_samples, jnp.swapaxes(top_transfer, 1, 2), root_sample


def solution(mesh):
    return jax.shard_map(
        functools.partial(on_device, mesh.shape["leaf"], mesh.shape["cols"]),
        mesh=mesh,
        in_specs=(
            P(None, "leaf"),
            P("cols", "leaf"),
            P(None, "cols"),
            P("leaf", None, None),
            P("leaf", None),
            P("leaf"),
            P("leaf", None),
        ),
        out_specs=(
            P("cols", "leaf"),
            P("cols", "leaf"),
            P(None, "leaf"),
            P("leaf", "cols"),
            P(),
            P(None, "cols"),
        ),
        check_vma=False,
    )
```

profile of v0, /device:TPU:1, one launch (start us, length us, event | category | flops | bytes accessed | tf_op | source)
XLA Modules:
  0.0 187.6 jit_solution(14844668223190971540)
XLA Ops:
  0.6 0.7 multiply_add_fusion.1
  1.3 0.1 copy.15
  1.4 0.1 stack.9
  1.5 0.1 copy.16
  1.6 0.1 stack.10
  1.7 0.0 copy-start.1
  1.7 0.9 copy-done.1
  2.7 0.8 copy-done.4
  3.4 69.1 %fetch.1 = (f32[64,144,128]{2,1,0:T(8,128)S(1)}, f32[576,128]{1,0:T(8,128)S(1)}, f32[2,24,128]{2,1,0:T(8,128)S(1)}) custom-call(f32[32,2048]{1,0:T(8,128)S(1)} %copy-done.1, f32[3,2048]{1,0:T(4,128)S(1)} %copy-done.4, s32[4,8,128]{2,1,0:T(8,128)S(1)} %pad.4.sent_requests), custom_call_target="tpu_custom_call" | custom-call | tf_op jit(solution)/shard_map/fetch/pallas_call | solution.py:204
  72.6 0.0 copy-start.5
  72.6 0.7 copy-done.5
  73.3 0.7 copy-done.6
  74.0 0.7 copy-done.7
  74.7 0.7 copy-done.8
  75.3 17.3 %sample.1 = (f32[32,2048]{1,0:T(8,128)}, f32[32,2048]{1,0:T(8,128)}, f32[32,2048]{1,0:T(8,128)S(1)}) custom-call(f32[64,144,128]{2,1,0:T(8,128)S(1)} %get-tuple-element.16.recv, f32[576,128]{1,0:T(8,128)S(1)} %get-tuple-element.17.local, f32[2,24,128]{2,1,0:T(8,128)S(1)} %get-tuple-element.18.halo, f32[3,2048]{1,0:T(4,128)S(1)} %copy-done.4, ...), custom_call_target="tpu_custom_call" | custom-call | tf_op jit(solution)/shard_map/sample/pallas_call | solution.py:351
  92.6 0.7 copy-done.3
  93.3 19.2 %total.1.sketched = f32[32,2048]{1,0:T(8,128)} custom-call(f32[32,2048]{1,0:T(8,128)} %copy-done.3), custom_call_target="tpu_custom_call" | custom-call | tf_op jit(solution)/shard_map/total/pallas_call | solution.py:405
  112.5 0.9 copy-done
  113.5 0.9 copy-done.2
  114.4 70.3 %tree.1 = (f32[32,2048]{1,0:T(8,128)S(1)}, f32[32,32]{1,0:T(8,128)S(1)}, f32[63,32,64]{2,1,0:T(8,128)S(1)}, f32[32,32]{1,0:T(8,128)S(1)}) custom-call(f32[32,2048]{1,0:T(8,128)S(1)} %copy-done, f32[32,2048]{1,0:T(8,128)S(1)} %copy-done.2), custom_call_target="tpu_custom_call" | custom-call | tf_op jit(solution)/shard_map/tree/pallas_call | solution.py:725
  184.7 0.7 copy.23
  185.4 0.6 copy.24
  186.0 1.0 copy.25
  186.9 0.6 copy.26
  (9 shorter events, 0.0 us)
Async XLA Ops:
  1.7 1.0 copy-start.1
  2.7 0.8 copy-start.4
  72.6 0.7 copy-start.5
  73.3 0.7 copy-start.6
  74.0 0.7 copy-start.7
  74.7 0.7 copy-start.8
  92.6 0.7 copy-start.3
  112.5 1.0 copy-start
  113.5 0.9 copy-start.2
where the time goes:
time: 188 us
  Pallas kernels  176 us (94%)
  local copies, waits for them, and re-layouts  10.3 us (5%)
    pallas_call x1, Pallas kernels, tree(): pl.pallas_call(functools.partial(tree_body, leaves, n_leaf, n_cols), out_...  70.3 us
    pallas_call x1, Pallas kernels, fetch(): pl.pallas_call(functools.partial(fetch_body, n_leaf), out_shape=(jax.Shap...  69.1 us
    pallas_call x1, Pallas kernels, total(): pl.pallas_call(functools.partial(total_body, n), out_shape=jax.ShapeDtype...  19.2 us
    pallas_call x1, Pallas kernels, sample(): pl.pallas_call(functools.partial(sample_body, leaves, n_leaf), out_shape=...  17.3 us
    unnamed x22, local copies, waits for them, and re-layouts  9.92 us

commit v1 on v0

--- a/solution.py
+++ b/solution.py
@@ -359,60 +359,6 @@
     )(recv, local, halo, points, slots, counts, near, sketch)
 
 
-def total_body(n, partial, out, parts, send_a, recv_a, send_b, recv_b):
-    me = lax.axis_index("cols")
-    width = partial.shape[1] // n
-    peers = [(me + k) % n for k in range(1, n)]
-    greet("cols", peers)
-
-    def piece(owner):
-        return pl.ds(pl.multiple_of(owner * width, width), width)
-
-    first = []
-    for k in range(1, n):
-        copy = pltpu.make_async_remote_copy(
-            src_ref=partial.at[:, piece(peers[k - 1])], dst_ref=parts.at[k - 1], send_sem=send_a.at[k - 1],
-            recv_sem=recv_a.at[k - 1], device_id={"cols": peers[k - 1]}, device_id_type=MESH,
-        )
-        copy.start()
-        first.append(copy)
-    value = partial[:, piece(me)]
-    for k in range(1, n):
-        first[k - 1].wait_recv()
-        value = value + parts[k - 1]
-    out[:, piece(me)] = value
-    second = []
-    for k in range(1, n):
-        copy = pltpu.make_async_remote_copy(
-            src_ref=out.at[:, piece(me)], dst_ref=out.at[:, piece(me)], send_sem=send_b.at[k - 1],
-            recv_sem=recv_b.at[k - 1], device_id={"cols": peers[k - 1]}, device_id_type=MESH,
-        )
-        copy.start()
-        second.append(copy)
-    for k in range(1, n):
-        owner = (me + n - k) % n
-        pltpu.make_async_remote_copy(
-            src_ref=out.at[:, piece(owner)], dst_ref=out.at[:, piece(owner)], send_sem=send_b.at[k - 1],
-            recv_sem=recv_b.at[k - 1], device_id={"cols": peers[k - 1]}, device_id_type=MESH,
-        ).wait_recv()
-    for copy in first + second:
-        copy.wait_send()
-
-
-def total(partial, n):
-    rows, columns = partial.shape
-    dma = pltpu.SemaphoreType.DMA
-    return pl.pallas_call(
-        functools.partial(total_body, n),
-        out_shape=jax.ShapeDtypeStruct(partial.shape, jnp.float32),
-        in_specs=[whole],
-        out_specs=whole,
-        scratch_shapes=[VMEM((n - 1, rows, columns // n), jnp.float32)] + [dma((n - 1,))] * 4,
-        compiler_params=pltpu.CompilerParams(collective_id=2, has_side_effects=True),
-        name="total",
-    )(partial)
-
-
 def eye(shape, first=0):
     rows = lax.broadcasted_iota(jnp.int32, shape, 0)
     return jnp.where(lanes(shape) == rows + first, 1.0, 0.0).astype(jnp.float32)
@@ -425,7 +371,7 @@
 
 
 def compress(tiles, traces):
-    block = 4 if len(tiles) > 8 else 8
+    block = 8
     shape = (RANK, 4 * RANK)
     on_diagonal = lanes(shape) == lax.broadcasted_iota(jnp.int32, shape, 0)
     tiles = [
@@ -495,237 +441,323 @@
     return dot_nn(left, jnp.concatenate([s_high, s_high, s_rest], axis=0), None)
 
 
-def level(read, write, count, group):
-    def some(start):
-        inputs = [read(start + b) for b in range(min(group, count))]
-        pairs = [parent_tile(c) for c, _ in inputs]
-        tiles = compress([tile for tile, _ in pairs], [trace for _, trace in pairs])
-        for b, (tile, (_, stacked)) in enumerate(zip(tiles, inputs)):
-            write(start + b, tile, project(tile, stacked))
-
-    if count <= group:
-        some(0)
-    else:
-        lax.fori_loop(0, count // group, lambda g, carry: (some(g * group), carry)[1], 0)
-
-
-def branch_body(leaves, sketched, far, basis, branch, packed_c, packed_p, nodes, projected):
-    low = lanes((RANK, 2 * LEAF)) < LEAF
+def parents(current):
+    pairs = [
+        parent_tile(pltpu.roll(jnp.concatenate(current[i : i + 2], axis=0), 3 * RANK, 1))
+        for i in range(0, len(current), 2)
+    ]
+    return compress([tile for tile, _ in pairs], [trace for _, trace in pairs])
+
+
+def chain(current):
+    levels = []
+    while len(current) > 1:
+        current = parents(current)
+        levels.append(current)
+    return levels
+
+
+def side_by_side(first, second):
+    return jnp.where(lanes(first.shape) < 2 * RANK, swap_halves(first), second)
+
+
+def descriptor(src, dst, send, recv, axis, peer):
+    return pltpu.make_async_remote_copy(
+        src_ref=src, dst_ref=dst, send_sem=send, recv_sem=recv, device_id={axis: peer}, device_id_type=MESH
+    )
+
+
+PARTS = ((0, 2), (2, 1), (3, 1))
+
+
+def subtree(n_cols, tiles, traces, out, send, recv):
+    col = lax.axis_index("cols")
+    others = [(col + k) % n_cols for k in range(1, n_cols)]
+    sent = []
+
+    def publish(part):
+        rows = pl.ds(*PARTS[part])
+        for k in range(n_cols - 1):
+            copy = descriptor(
+                out.at[col, rows], out.at[col, rows], send.at[part, k], recv.at[part, k], "cols", others[k]
+            )
+            copy.start()
+            sent.append(copy)
+
+    current = compress(tiles, traces)
+    out[col, 0] = side_by_side(current[0], current[1])
+    out[col, 1] = side_by_side(current[2], current[3])
+    publish(0)
+    current = parents(current)
+    out[col, 2] = side_by_side(current[0], current[1])
+    publish(1)
+    out[col, 3] = parents(current)[0]
+    publish(2)
+
+    def collect(part):
+        rows = pl.ds(*PARTS[part])
+        for k in range(n_cols - 1):
+            owner = (col + n_cols - k - 1) % n_cols
+            descriptor(
+                out.at[owner, rows], out.at[owner, rows], send.at[part, k], recv.at[part, k], "cols", others[k]
+            ).wait_recv()
+
+    def end():
+        for copy in sent:
+            copy.wait_send()
+
+    return collect, end
+
+
+def leaf_body(n_cols, partial, out, pieces, send_a, recv_a, send_b, recv_b):
+    me = lax.axis_index("cols")
+    width = partial.shape[1] // n_cols
+    peers = [(me + k) % n_cols for k in range(1, n_cols)]
+    greet("cols", peers)
+
+    def piece(owner):
+        return pl.ds(pl.multiple_of(owner * width, width), width)
+
+    first = []
+    for k in range(1, n_cols):
+        copy = descriptor(
+            partial.at[:, piece(peers[k - 1])], pieces.at[k - 1], send_a.at[k - 1], recv_a.at[k - 1], "cols", peers[k - 1]
+        )
+        copy.start()
+        first.append(copy)
+    value = partial[:, piece(me)]
+    for k in range(1, n_cols):
+        first[k - 1].wait_recv()
+        value = value + pieces[k - 1]
     unit = eye((2 * RANK, 2 * RANK))
-    group = 16
-
-    def project_t(tile, row):
-        high, rest = [part.astype(jnp.float32) for part in halves(tile)]
-        r_high, r_rest = [part.astype(jnp.float32) for part in halves(row)]
-        left = [jnp.where(low, swap_halves(rest), high), jnp.where(low, 0.0, high)]
-        right = [jnp.where(low, swap_halves(r_high), r_high), r_rest]
-        return dot_nt(
-            jnp.concatenate(left, axis=1).astype(jnp.bfloat16), jnp.concatenate(right, axis=1).astype(jnp.bfloat16), None
-        )
-
-    def some(g, carry):
-        bs, rows = [], []
-        for j in range(group // 2):
-            at = pl.ds(pl.multiple_of((g * (group // 2) + j) * 2 * LEAF, 2 * LEAF), 2 * LEAF)
-            b, row = sketched[:, at], far[:, at]
-            bs += [b[:, :LEAF], swap_halves(b)[:, :LEAF]]
-            rows += [swap_halves(row), row]
-        tiles = compress([dot_nt(b, jnp.concatenate([b, b, unit], axis=0)) for b in bs], [total_of(b * b) for b in bs])
-        for b, (tile, row) in enumerate(zip(tiles, rows)):
-            nodes[g * group + b] = tile
-            projected[g * group + b] = project_t(tile, row)
-        for j in range(group // 2):
-            at = pl.ds(pl.multiple_of((g * (group // 2) + j) * 2 * LEAF, 2 * LEAF), 2 * LEAF)
-            basis[:, at] = jnp.where(low, swap_halves(tiles[2 * j]), tiles[2 * j + 1])
-        return carry
-
-    lax.fori_loop(0, leaves // group, some, 0)
-
-    def read(node):
-        pair = nodes[pl.ds(2 * node, 2)].reshape(2 * RANK, 4 * RANK)
-        return pltpu.roll(pair, 3 * RANK, 1), projected[pl.ds(2 * node, 2)].reshape(2 * RANK, RANK)
-
-    def write(node, tile, value):
-        nodes[node] = tile
-        projected[node] = value
-
-    count = leaves // 2
-    while count >= 1:
-        level(read, write, count, 16)
-        count //= 2
-    branch[...] = projected[0]
+    bs = []
+    for j in range(2):
+        pair = value[:, 2 * LEAF * j : 2 * LEAF * (j + 1)]
+        bs += [pair[:, :LEAF], swap_halves(pair)[:, :LEAF]]
+    tiles = [dot_nt(b, jnp.concatenate([b, b, unit], axis=0)) for b in bs]
+    collect, end = subtree(n_cols, tiles, [total_of(b * b) for b in bs], out, send_b, recv_b)
+    for part in range(3):
+        collect(part)
+    for copy in first:
+        copy.wait_send()
+    end()
+
+
+def leaf_tiles(partial, n_cols):
+    rows, columns = partial.shape
+    dma = pltpu.SemaphoreType.DMA
+    return pl.pallas_call(
+        functools.partial(leaf_body, n_cols),
+        out_shape=jax.ShapeDtypeStruct((n_cols, 4, RANK, 4 * RANK), jnp.float32),
+        in_specs=[whole],
+        out_specs=whole,
+        scratch_shapes=[VMEM((n_cols - 1, rows, columns // n_cols), jnp.float32)]
+        + [dma((n_cols - 1,))] * 2
+        + [dma((3, n_cols - 1))] * 2,
+        compiler_params=pltpu.CompilerParams(collective_id=2, has_side_effects=True, vmem_limit_bytes=40 * MIB),
+        name="leaf_tiles",
+    )(partial)
+
+
+def unpack(block):
+    return jnp.concatenate([pltpu.roll(block, (4 * RANK - RANK * g) % (4 * RANK), 1) for g in range(4)], axis=0)
+
+
+def pack(source, shift):
     quarter = lanes((8, 4 * RANK)) // RANK
-    wide = dot_nn(projected[0], eye((RANK, 4 * RANK)))
-    tile = nodes[0]
-    for i, (source, shift) in enumerate(((tile, RANK), (wide, 0))):
-        row = jnp.zeros((8, 4 * RANK), jnp.float32)
-        for g in range(4):
-            turned = pltpu.roll(source[8 * g : 8 * g + 8], (RANK * g - shift) % (4 * RANK), 1)
-            row = jnp.where(quarter == g, turned, row)
-        if i == 0:
-            for g in range(8):
-                packed_c[g] = row[g : g + 1]
-        else:
-            packed_p[...] = row
-
-
-def meet(n_leaf, n_cols):
+    row = jnp.zeros((8, 4 * RANK), jnp.float32)
+    for g in range(4):
+        turned = pltpu.roll(source[8 * g : 8 * g + 8], (RANK * g - shift) % (4 * RANK), 1)
+        row = jnp.where(quarter == g, turned, row)
+    return row
+
+
+def project_t(tile, row):
+    low = lanes(tile.shape) < LEAF
+    high, rest = [part.astype(jnp.float32) for part in halves(tile)]
+    r_high, r_rest = [part.astype(jnp.float32) for part in halves(row)]
+    left = [jnp.where(low, swap_halves(rest), high), jnp.where(low, 0.0, high)]
+    right = [jnp.where(low, swap_halves(r_high), r_high), r_rest]
+    return dot_nt(
+        jnp.concatenate(left, axis=1).astype(jnp.bfloat16), jnp.concatenate(right, axis=1).astype(jnp.bfloat16), None
+    )
+
+
+def both(pair):
+    return [swap_halves(pair), pair]
+
+
+def climb(tiles, owner, values):
+    second = both(tiles[owner, 2])
+    values = [project(second[i], jnp.concatenate(values[2 * i : 2 * i + 2], axis=0)) for i in range(2)]
+    return project(tiles[owner, 3], jnp.concatenate(values, axis=0))
+
+
+def finish(levels, values):
+    for tiles in levels:
+        values = [project(tile, jnp.concatenate(values[2 * i : 2 * i + 2], axis=0)) for i, tile in enumerate(tiles)]
+    return values[0]
+
+
+def tree_body(
+    n_leaf, n_cols, tiles, far, basis, branch, transfers, root,
+    upper, samples, top_samples, chosen, packed_p, out_p,
+    yc_send, yc_recv, zc_send, zc_recv, yp_send, yp_recv, zp_send, zp_recv, x_send, x_recv, own,
+):
     n_y = ROWS_Y
     n_z = n_leaf // n_y
+    seg = n_leaf // n_cols
     me, col = lax.axis_index("leaf"), lax.axis_index("cols")
     y, z = me // n_z, me % n_z
     across = [((y + k) % n_y) * n_z + z for k in range(1, n_y)]
     along = [y * n_z + (z + k) % n_z for k in range(1, n_z)]
     others = [(col + k) % n_cols for k in range(1, n_cols)]
+    far_first = sorted(range(n_z - 1), key=lambda k: -min(k + 1, n_z - 1 - k))
     barrier = pltpu.get_barrier_semaphore()
     for peer in across + along:
         pl.semaphore_signal(barrier, inc=1, device_id={"leaf": peer}, device_id_type=MESH)
     for peer in others:
         pl.semaphore_signal(barrier, inc=1, device_id={"cols": peer}, device_id_type=MESH)
-    return lambda: pl.semaphore_wait(barrier, len(across) + len(along) + len(others))
-
-
-def gather_body(n_leaf, n_cols, packed_c, packed_p, out_c, out_p, sems):
-    yc_send, yc_recv, yp_send, yp_recv, zc_send, zc_recv, zp_send, zp_recv, x_send, x_recv, own = sems
-    n_y = ROWS_Y
-    n_z = n_leaf // n_y
-    me, col = lax.axis_index("leaf"), lax.axis_index("cols")
-    y, z = me // n_z, me % n_z
-    across = [((y + k) % n_y) * n_z + z for k in range(1, n_y)]
-    along = [y * n_z + (z + k) % n_z for k in range(1, n_z)]
-    others = [(col + k) % n_cols for k in range(1, n_cols)]
-    sent = []
-
-    def push(src, dst, send, recv, axis, peer):
-        copy = pltpu.make_async_remote_copy(
-            src_ref=src, dst_ref=dst, send_sem=send, recv_sem=recv, device_id={axis: peer}, device_id_type=MESH
-        )
+
+    levels = chain([tiles[c, 3] for c in range(n_cols)])
+    packed_c = pack(levels[-1][0], RANK)
+    pl.semaphore_wait(barrier, len(across) + len(along) + len(others))
+
+    tree_y, tree_z = (col * seg) // n_z, (col * seg) % n_z
+    slot = z % seg
+    carries = z // seg == tree_z // seg
+    starts = carries & (y == tree_y)
+
+    def c_across(k):
+        return descriptor(chosen.at[slot], chosen.at[slot], yc_send.at[k], yc_recv, "leaf", across[k])
+
+    def c_along(k):
+        return descriptor(chosen.at[slot], chosen.at[slot], zc_send.at[k], zc_recv.at[slot], "leaf", along[k])
+
+    @pl.when(starts)
+    def _():
+        chosen[slot] = packed_c
+        for k in range(n_y - 1):
+            c_across(k).start()
+
+    def lower(g, carry):
+        owners = [4 * g + b for b in range(4)]
+        values = []
+        for c in owners:
+            leaves = []
+            for j in range(2):
+                at = pl.ds(pl.multiple_of((2 * c + j) * 2 * LEAF, 2 * LEAF), 2 * LEAF)
+                pair, rows = tiles[c, j], far[:, at]
+                basis[:, at] = pair
+                leaves += [project_t(q, row) for q, row in zip(both(pair), both(rows))]
+            values.append(leaves)
+        for c, leaves in zip(owners, values):
+            samples[c] = climb(tiles, c, leaves)
+        return carry
+
+    lax.fori_loop(0, n_cols // 4, lower, 0)
+    value = finish(levels, [samples[c] for c in range(n_cols)])
+    branch[...] = value
+    packed_p[...] = pack(jnp.concatenate([value, jnp.zeros((RANK, 3 * RANK), jnp.float32)], axis=1), 0)
+
+    p_across = [
+        descriptor(packed_p, out_p.at[z, y], yp_send.at[k], yp_recv.at[k], "leaf", across[k]) for k in range(n_y - 1)
+    ]
+    for copy in p_across:
         copy.start()
-        sent.append(copy)
-
-    def arrived(ref, send, recv, axis, peer):
-        pltpu.make_async_remote_copy(
-            src_ref=ref, dst_ref=ref, send_sem=send, recv_sem=recv, device_id={axis: peer}, device_id_type=MESH
-        ).wait_recv()
-
+    mine = pltpu.make_async_copy(packed_p, out_p.at[z, y], own)
+    mine.start()
+
+    @pl.when(carries & (y != tree_y))
+    def _():
+        c_across(0).wait_recv()
+
+    @pl.when(carries)
+    def _():
+        for k in far_first:
+            c_along(k).start()
+
+    mine.wait()
     for k in range(n_y - 1):
-        push(packed_c.at[col], out_c.at[col, z, y], yc_send.at[k], yc_recv.at[k], "leaf", across[k])
-    for k in range(n_y - 1):
-        push(packed_p, out_p.at[z, y], yp_send.at[k], yp_recv.at[k], "leaf", across[k])
-    mine = [
-        pltpu.make_async_copy(packed_c.at[col], out_c.at[col, z, y], own.at[0]),
-        pltpu.make_async_copy(packed_p, out_p.at[z, y], own.at[1]),
+        other = (y + n_y - k - 1) % n_y
+        descriptor(packed_p, out_p.at[z, other], yp_send.at[k], yp_recv.at[k], "leaf", across[k]).wait_recv()
+    p_along = [
+        descriptor(out_p.at[z], out_p.at[z], zp_send.at[k], zp_recv.at[k], "leaf", along[k]) for k in range(n_z - 1)
     ]
-    for copy in mine:
-        copy.start()
-    for copy in mine:
-        copy.wait()
-    far_first = sorted(range(n_z - 1), key=lambda k: -min(k + 1, n_z - 1 - k))
-    for k in range(n_y - 1):
-        arrived(out_c.at[col, z, (y + n_y - k - 1) % n_y], yc_send.at[k], yc_recv.at[k], "leaf", across[k])
     for k in far_first:
-        push(out_c.at[col, z], out_c.at[col, z], zc_send.at[k], zc_recv.at[k], "leaf", along[k])
-    for k in range(n_y - 1):
-        arrived(out_p.at[z, (y + n_y - k - 1) % n_y], yp_send.at[k], yp_recv.at[k], "leaf", across[k])
-    for k in far_first:
-        push(out_p.at[z], out_p.at[z], zp_send.at[k], zp_recv.at[k], "leaf", along[k])
+        p_along[k].start()
+
+    for i in range(seg):
+
+        @pl.when(tree_z + i != z)
+        def _():
+            descriptor(chosen.at[i], chosen.at[i], zc_send.at[i], zc_recv.at[i], "leaf", along[0]).wait_recv()
+
+    pairs = [
+        parent_tile(jnp.concatenate([unpack(chosen[2 * i]), unpack(chosen[2 * i + 1])], axis=0)) for i in range(seg // 2)
+    ]
+    collect, end = subtree(n_cols, [tile for tile, _ in pairs], [trace for _, trace in pairs], upper, x_send, x_recv)
+    collect(2)
+    levels = chain([upper[c, 3] for c in range(n_cols)])
+    collect(0)
+    collect(1)
     for k in range(n_z - 1):
-        arrived(out_c.at[col, (z + n_z - k - 1) % n_z], zc_send.at[k], zc_recv.at[k], "leaf", along[k])
-    for k in range(n_cols - 1):
-        push(out_c.at[col], out_c.at[col], x_send.at[k], x_recv.at[k], "cols", others[k])
-    for k in range(n_cols - 1):
-        arrived(out_c.at[(col + n_cols - k - 1) % n_cols], x_send.at[k], x_recv.at[k], "cols", others[k])
-
-    def later():
+        other = (z + n_z - k - 1) % n_z
+        descriptor(out_p.at[other], out_p.at[other], zp_send.at[k], zp_recv.at[k], "leaf", along[k]).wait_recv()
+
+    def q_of(tile):
+        return tile[:, : 2 * RANK]
+
+    def higher(g, carry):
+        owners = [4 * g + b for b in range(4)]
+        values = []
+        for c in owners:
+            nodes = []
+            for j in range(2):
+                for i, tile in enumerate(both(upper[c, j])):
+                    at = c * seg + 2 * (2 * j + i)
+                    children = [unpack(out_p[(at + d) % n_z, (at + d) // n_z]) for d in range(2)]
+                    nodes.append(project(tile, jnp.concatenate(children, axis=0)))
+                    transfers[4 * c + 2 * j + i] = q_of(swap_halves(tile))
+            values.append(nodes)
+        for c, nodes in zip(owners, values):
+            for i, tile in enumerate(both(upper[c, 2])):
+                transfers[4 * n_cols + 2 * c + i] = q_of(swap_halves(tile))
+            transfers[6 * n_cols + c] = q_of(swap_halves(upper[c, 3]))
+            top_samples[c] = climb(upper, c, nodes)
+        return carry
+
+    lax.fori_loop(0, n_cols // 4, higher, 0)
+    first = 7 * n_cols
+    for level_tiles in levels:
+        for i, tile in enumerate(level_tiles):
+            transfers[first + i] = q_of(swap_halves(tile))
+        first += len(level_tiles)
+    root[...] = finish(levels, [top_samples[c] for c in range(n_cols)])[:, :RANK]
+
+    @pl.when(starts)
+    def _():
+        for k in range(n_y - 1):
+            c_across(k).wait_send()
+
+    @pl.when(carries)
+    def _():
         for k in range(n_z - 1):
-            arrived(out_p.at[(z + n_z - k - 1) % n_z], zp_send.at[k], zp_recv.at[k], "leaf", along[k])
-
-    def end():
-        for copy in sent:
-            copy.wait_send()
-
-    return later, end
-
-
-def top_body(n_leaf, gathered_c, gathered_p, transfers, root, nodes, projected, later):
-    n_z = n_leaf // ROWS_Y
-    count = n_leaf // 2
-
-    def unpack(block):
-        return jnp.concatenate([pltpu.roll(block, (4 * RANK - RANK * g) % (4 * RANK), 1) for g in range(4)], axis=0)
-
-    def children(node):
-        return [(child % n_z, child // n_z) for child in (2 * node, 2 * node + 1)]
-
-    def first_level(g, carry):
-        stacked = []
-        for b in range(16):
-            pair = children(16 * g + b)
-            stacked.append(
-                jnp.concatenate(
-                    [unpack(jnp.concatenate([gathered_c[i, z, y] for i in range(8)], axis=0)) for z, y in pair], axis=0
-                )
-            )
-        pairs = [parent_tile(c) for c in stacked]
-        tiles = compress([tile for tile, _ in pairs], [trace for _, trace in pairs])
-        for b in range(16):
-            nodes[16 * g + b] = tiles[b]
-            transfers[16 * g + b] = swap_halves(tiles[b])[:, : 2 * RANK]
-        return carry
-
-    lax.fori_loop(0, count // 16, first_level, 0)
-    later()
-
-    def first_projections(g, carry):
-        for b in range(16):
-            node = 16 * g + b
-            stacked = jnp.concatenate([unpack(gathered_p[z, y]) for z, y in children(node)], axis=0)
-            projected[node] = project(nodes[node], stacked)
-        return carry
-
-    lax.fori_loop(0, count // 16, first_projections, 0)
-
-    def read(node):
-        pair = nodes[pl.ds(2 * node, 2)].reshape(2 * RANK, 4 * RANK)
-        return pltpu.roll(pair, 3 * RANK, 1), projected[pl.ds(2 * node, 2)].reshape(2 * RANK, 4 * RANK)
-
-    first = count
-    count //= 2
-    while count >= 1:
-
-        def write(node, tile, value, first=first):
-            nodes[node] = tile
-            projected[node] = value
-            transfers[first + node] = swap_halves(tile)[:, : 2 * RANK]
-
-        level(read, write, count, 16)
-        first += count
-        count //= 2
-    root[...] = projected[0][:, :RANK]
-
-
-def tree_body(
-    leaves, n_leaf, n_cols, sketched, far, basis, branch, transfers, root,
-    nodes, projected, upper, packed_c, packed_p, out_c, out_p, *sems,
-):
-    wait = meet(n_leaf, n_cols)
-    branch_body(leaves, sketched, far, basis, branch, packed_c, packed_p, nodes, projected)
-    wait()
-    later, end = gather_body(n_leaf, n_cols, packed_c, packed_p, out_c, out_p, sems)
-    top_body(n_leaf, out_c, out_p, transfers, root, nodes, upper, later)
+            c_along(k).wait_send()
+
+    for copy in p_across + p_along:
+        copy.wait_send()
     end()
 
 
-def tree(sketched, far, n_leaf, n_cols):
-    leaves = sketched.shape[1] // LEAF
+def tree(tiles, far, n_leaf, n_cols):
     n_z = n_leaf // ROWS_Y
     f32 = jnp.float32
     dma = pltpu.SemaphoreType.DMA
-    count = max(leaves, n_leaf // 2)
     return pl.pallas_call(
-        functools.partial(tree_body, leaves, n_leaf, n_cols),
+        functools.partial(tree_body, n_leaf, n_cols),
         out_shape=(
-            jax.ShapeDtypeStruct(sketched.shape, f32),
+            jax.ShapeDtypeStruct(far.shape, f32),
             jax.ShapeDtypeStruct((RANK, RANK), f32),
             jax.ShapeDtypeStruct((n_leaf - 1, RANK, 2 * RANK), f32),
             jax.ShapeDtypeStruct((RANK, RANK), f32),
@@ -733,23 +765,29 @@
         in_specs=[whole, whole],
         out_specs=(whole, whole, whole, whole),
         scratch_shapes=[
-            VMEM((count, RANK, 4 * RANK), f32),
-            VMEM((leaves, RANK, RANK), f32),
-            VMEM((n_leaf // 2, RANK, 4 * RANK), f32),
-            VMEM((8, 1, 4 * RANK), f32),
+            VMEM((n_cols, 4, RANK, 4 * RANK), f32),
+            VMEM((n_cols, RANK, RANK), f32),
+            VMEM((n_cols, RANK, 4 * RANK), f32),
+            VMEM((n_leaf // n_cols, 8, 4 * RANK), f32),
             VMEM((8, 4 * RANK), f32),
-            VMEM((8, n_z, ROWS_Y, 1, 4 * RANK), f32),
             VMEM((n_z, ROWS_Y, 8, 4 * RANK), f32),
-        ]
-        + [dma((ROWS_Y - 1,))] * 4
-        + [dma((n_z - 1,))] * 4
-        + [dma((n_cols - 1,))] * 2
-        + [dma((2,))],
+            dma((ROWS_Y - 1,)),
+            dma,
+            dma((n_z - 1,)),
+            dma((n_leaf // n_cols,)),
+            dma((ROWS_Y - 1,)),
+            dma((ROWS_Y - 1,)),
+            dma((n_z - 1,)),
+            dma((n_z - 1,)),
+            dma((3, n_cols - 1)),
+            dma((3, n_cols - 1)),
+            dma,
+        ],
         compiler_params=pltpu.CompilerParams(
             collective_id=3, has_side_effects=True, vmem_limit_bytes=40 * MIB
         ),
         name="tree",
-    )(sketched, far)
+    )(tiles, far)
 
 
 def on_device(n_leaf, n_cols, points, samples, sketch, far_requests, far_slots, far_count, near_mask):
@@ -757,8 +795,8 @@
     far_sample, near_sample, partial = sample(
         recv, local, halo, points, far_slots.T, far_count, near_mask.T, sketch, n_leaf
     )
-    sketched = total(partial, n_cols)
-    leaf_basis, branch_samples, top_transfer, root_sample = tree(sketched, far_sample, n_leaf, n_cols)
+    tiles = leaf_tiles(partial, n_cols)
+    leaf_basis, branch_samples, top_transfer, root_sample = tree(tiles, far_sample, n_leaf, n_cols)
     return far_sample, near_sample, leaf_basis, branch_samples, jnp.swapaxes(top_transfer, 1, 2), root_sample
 
 

time: 188 us -> 161 us (0.86)
  Pallas kernels: 176 us -> 150 us
    pallas_call x2, Pallas kernels: 89.4 us -> 63.2 us  [the longest x1 38 us: tree(): pl.pallas_call(functools.partial(tree_body, n_leaf, n_cols), out_shape=(j...]
    unnamed x22 -> x18, local copies, waits for them, and re-layouts: 9.92 us -> 8.27 us
where the time goes in v1:
time: 161 us; the launch traced here: 160 us
  Pallas kernels  150 us (93%)
  local copies, waits for them, and re-layouts  8.63 us (5%)
    pallas_call x1, Pallas kernels, fetch(): pl.pallas_call(functools.partial(fetch_body, n_leaf), out_shape=(jax.Shap...  69.1 us
    pallas_call x1, Pallas kernels, tree(): pl.pallas_call(functools.partial(tree_body, n_leaf, n_cols), out_shape=(j...  38 us
    pallas_call x1, Pallas kernels, leaf_tiles(): pl.pallas_call(functools.partial(leaf_body, n_cols), out_shape=jax.ShapeD...  25.2 us
    pallas_call x1, Pallas kernels, sample(): pl.pallas_call(functools.partial(sample_body, leaves, n_leaf), out_shape=...  17.7 us
    unnamed x18, local copies, waits for them, and re-layouts  8.27 us

profile of v1, /device:TPU:1, one launch (start us, length us, event | category | flops | bytes accessed | tf_op | source)
XLA Modules:
  0.0 160.1 jit_solution(7408715522466912000)
XLA Ops:
  0.6 0.7 multiply_add_fusion.1
  1.3 0.1 copy.15
  1.4 0.1 stack.9
  1.5 0.1 copy.16
  1.6 0.1 stack.10
  1.7 0.0 copy-start.1
  1.7 0.9 copy-done.1
  2.7 0.0 copy-start.2
  2.7 0.8 copy-done.2
  3.4 69.1 %fetch.1 = (f32[64,144,128]{2,1,0:T(8,128)S(1)}, f32[576,128]{1,0:T(8,128)S(1)}, f32[2,24,128]{2,1,0:T(8,128)S(1)}) custom-call(f32[32,2048]{1,0:T(8,128)S(1)} %copy-done.1, f32[3,2048]{1,0:T(4,128)S(1)} %copy-done.2, s32[4,8,128]{2,1,0:T(8,128)S(1)} %pad.4.sent_requests), custom_call_target="tpu_custom_call" | custom-call | tf_op jit(solution)/shard_map/fetch/pallas_call | solution.py:204
  72.6 0.0 copy-start.3
  72.6 0.7 copy-done.3
  73.3 0.7 copy-done.4
  74.0 0.7 copy-done.5
  74.7 0.7 copy-done.6
  75.3 17.7 %sample.1 = (f32[32,2048]{1,0:T(8,128)}, f32[32,2048]{1,0:T(8,128)}, f32[32,2048]{1,0:T(8,128)S(1)}) custom-call(f32[64,144,128]{2,1,0:T(8,128)S(1)} %get-tuple-element.16.recv, f32[576,128]{1,0:T(8,128)S(1)} %get-tuple-element.17.local, f32[2,24,128]{2,1,0:T(8,128)S(1)} %get-tuple-element.18.halo, f32[3,2048]{1,0:T(4,128)S(1)} %copy-done.2, ...), custom_call_target="tpu_custom_call" | custom-call | tf_op jit(solution)/shard_map/sample/pallas_call | solution.py:351
  93.0 25.2 %leaf_tiles.1.tiles = f32[8,4,32,128]{3,2,1,0:T(8,128)S(1)} custom-call(f32[32,2048]{1,0:T(8,128)S(1)} %get-tuple-element.21.partial), custom_call_target="tpu_custom_call" | custom-call | tf_op jit(solution)/shard_map/leaf_tiles/pallas_call | solution.py:549
  118.2 0.0 copy-start
  118.2 0.9 copy-done
  119.2 38.0 %tree.1 = (f32[32,2048]{1,0:T(8,128)S(1)}, f32[32,32]{1,0:T(8,128)S(1)}, f32[63,32,64]{2,1,0:T(8,128)S(1)}, f32[32,32]{1,0:T(8,128)S(1)}) custom-call(f32[8,4,32,128]{3,2,1,0:T(8,128)S(1)} %leaf_tiles.1.tiles, f32[32,2048]{1,0:T(8,128)S(1)} %copy-done), custom_call_target="tpu_custom_call" | custom-call | tf_op jit(solution)/shard_map/tree/pallas_call | solution.py:757
  157.2 0.7 copy.23
  157.9 0.6 copy.24
  158.5 1.0 copy.25
  159.5 0.6 copy.26
  (5 shorter events, 0.0 us)
Async XLA Ops:
  1.7 1.0 copy-start.1
  2.7 0.8 copy-start.2
  72.6 0.7 copy-start.3
  73.3 0.7 copy-start.4
  74.0 0.7 copy-start.5
  74.7 0.7 copy-start.6
  118.2 1.0 copy-start

commit v2 on v1

--- a/solution.py
+++ b/solution.py
@@ -12,6 +12,9 @@
 CAP = 8
 RANK = 32
 NEAR = 3
+SLOT_ROW = CAP
+MASK_ROW = SLOT_ROW + FAR
+COUNT_ROW = MASK_ROW + NEAR
 ROWS_Y = 4
 CELL = 16
 HALF = 16
@@ -25,7 +28,6 @@
 MESH = pl.DeviceIdType.MESH
 VMEM = pltpu.VMEM
 whole = pl.BlockSpec(memory_space=pltpu.VMEM)
-scalars = pl.BlockSpec(memory_space=pltpu.SMEM)
 MIB = 1 << 20
 
 
@@ -47,6 +49,55 @@
     return lax.dot_general(
         a, b, (((1,), (0,)), ((), ())), precision=precision, preferred_element_type=jnp.float32
     )
+
+
+def halves(value):
+    high = value.astype(jnp.bfloat16)
+    return high, (value - high.astype(jnp.float32)).astype(jnp.bfloat16)
+
+
+def columns_of(both):
+    both = jnp.concatenate([both, jnp.zeros((5, 2 * LEAF), jnp.float32)], axis=0).T
+    return [
+        [jnp.broadcast_to(block[:, a : a + 1], (LEAF, 2 * LEAF)) for a in range(3)] for block in (both[:LEAF], both[LEAF:])
+    ]
+
+
+def pair_of_clusters(coordinates, first, second):
+    (block_a, row_a, last_a, scale_a), (block_b, row_b, last_b, scale_b) = first, second
+    low16 = lanes((CELL, 2 * LEAF)) < LEAF
+    low1 = lanes((1, 2 * LEAF)) < LEAF
+    x = jnp.where(low1, row_a, swap_halves(row_b))
+    y = jnp.where(low1, swap_halves(row_a), row_b)
+    z = jnp.where(low1, last_a, last_b)
+    dx = coordinates[0] - x
+    dy = coordinates[1] - y
+    dz = coordinates[2] - z
+    square = dx * dx + dy * dy + dz * dz
+    values = jnp.exp2(square * lax.rsqrt(jnp.maximum(square, 1e-30)) * (-1.4426950408889634 / length_scale))
+    block_a = block_a * scale_a
+    block_b = block_b * scale_b
+    rows = jnp.concatenate(
+        [jnp.where(low16, block_a, swap_halves(block_b)), jnp.where(low16, swap_halves(block_a), block_b)], axis=0
+    )
+    return halves(values), halves(rows)
+
+
+def four(coordinates, entries):
+    (k0h, k0l), (s0h, s0l) = pair_of_clusters(coordinates, entries[0], entries[1])
+    (k1h, k1l), (s1h, s1l) = pair_of_clusters(coordinates, entries[2], entries[3])
+    left = jnp.concatenate([jnp.concatenate([s0h, s1h], axis=1), jnp.concatenate([s0l, s1l], axis=1)], axis=0)
+    right = jnp.concatenate([jnp.concatenate([k0h, k1h], axis=1), jnp.concatenate([k0l, k1l], axis=1)], axis=0)
+    return left, right
+
+
+def fold(total):
+    total = total[: 2 * CELL] + total[2 * CELL :]
+    return total + swap_halves(total)
+
+
+def two(first, second):
+    return jnp.where(lanes((2 * CELL, 2 * LEAF)) < LEAF, fold(first), fold(second))
 
 
 def greet(axis, peers):
@@ -57,19 +108,24 @@
 
 
 def fetch_body(
-    n_leaf, samples, points, sent_requests, recv, local, halo, *scratch
+    n_leaf, samples, points, table, recv, close, *scratch
 ):
     n_y = ROWS_Y
     n_z = n_leaf // n_y
-    chunks = (local,) + scratch[: n_z - 1]
-    stage, edge, asked_v, asked, ring_send, ring_recv, y_send, y_recv, q_send, q_recv, q_local, e_send, e_recv = scratch[n_z - 1 :]
+    chunks = scratch[:n_z]
+    local = chunks[0]
+    scalars, cells, halo, stage, edge, asked_v, asked, ring_send, ring_recv, y_send, y_recv, q_send, q_recv, q_local, e_send, e_recv, start_sem = scratch[n_z:]
     me = lax.axis_index("leaf")
     y, z = me // n_z, me % n_z
     up = y * n_z + (z + 1) % n_z
     down = y * n_z + (z + n_z - 1) % n_z
     above, below = (me + 1) % n_leaf, (me + n_leaf - 1) % n_leaf
     across = [None] + [((y + k) % n_y) * n_z + z for k in range(1, n_y)]
+    leaves = samples.shape[1] // LEAF
+    read = pltpu.make_async_copy(table, scalars, start_sem)
+    read.start()
     greet("leaf", [up, down, above, below] + across[1:])
+    own = table.at[pl.ds(0, CAP)]
 
     def remote(src, dst, send, recv_sem, peer):
         return pltpu.make_async_remote_copy(
@@ -81,7 +137,7 @@
     asks = []
     for k in range(1, n_y):
         copy = remote(
-            sent_requests.at[(y + k) % n_y], asked_v.at[n_y - k - 1], q_send.at[k - 1], q_recv.at[n_y - k - 1], across[k]
+            own, asked_v.at[n_y - k - 1], q_send.at[k - 1], q_recv.at[n_y - k - 1], across[k]
         )
         copy.start()
         asks.append(copy)
@@ -139,18 +195,17 @@
 
     for copy in asks:
         copy.wait_recv()
-    moves = [
-        pltpu.make_async_copy(asked_v, asked.at[pl.ds(1, n_y - 1)], q_local.at[0]),
-        pltpu.make_async_copy(sent_requests.at[y], asked.at[0], q_local.at[1]),
-    ]
-    for move in moves:
-        move.start()
+    moves = [read, pltpu.make_async_copy(asked_v, asked, q_local)]
+    moves[1].start()
     for move in moves:
         move.wait()
 
     def pick(chunk, target, request):
         def one(c, carry):
-            cell, row = request(c)
+            cluster = request(c)
+            upper = cluster >> (HALF.bit_length() - 1)
+            cell = cluster + upper * (SUB // CELL - HALF)
+            row = HALF * CELL + cluster * 2 + upper * (SUB - 2 * HALF)
             target[pl.ds(pl.multiple_of(c * CELL, CELL), CELL), :] = chunk[pl.ds(cell * CELL, CELL), :]
             for part in range(2):
                 target[pl.ds(CAP * CELL + c * 2 + part, 1), :] = chunk[pl.ds(row + part, 1), :]
@@ -165,7 +220,7 @@
         source_z = (z + n_z - slot) % n_z
 
         def requests(k):
-            return lambda c: (asked[k, 0, source_z * CAP + c], asked[k, 1, source_z * CAP + c])
+            return lambda c: (asked[k - 1, c, y * n_z + source_z] if k else scalars[c, y * n_z + source_z])
 
         for k in range(1, n_y):
             pick(chunk, stage.at[k - 1, slot], requests(k))
@@ -177,6 +232,42 @@
             arriving.append(copy)
         pick(chunk, recv.at[slot], requests(0))
 
+    for c in range(leaves):
+        base = (c // HALF) * SUB + (c % HALF) * CELL
+        cbase = (c // HALF) * SUB + HALF * CELL + (c % HALF) * 2
+        cells[c + 1, 0:CELL, :] = local[base : base + CELL, :]
+        cells[c + 1, CELL : CELL + 2, :] = local[cbase : cbase + 2, :]
+
+    def near_entry(leaf, offset):
+        if offset < NEAR:
+            place = me * leaves + leaf + offset - NEAR // 2
+            inside = (place >= 0) & (place < n_leaf * leaves)
+            scale = (scalars[MASK_ROW + offset, leaf] * inside.astype(jnp.int32)).astype(jnp.float32)
+        else:
+            scale = jnp.float32(0)
+        at = leaf + offset if offset < NEAR else leaf
+        return cells[at, 0:CELL, :], cells[at, CELL : CELL + 1, :], cells[at, CELL + 1 : CELL + 2, :], scale
+
+    def near_pair(j, carry):
+        at = pl.ds(pl.multiple_of(j * 2 * LEAF, 2 * LEAF), 2 * LEAF)
+        coordinates = columns_of(points[:, at])
+        totals = []
+        for i in range(2):
+            left, right = four(coordinates[i], [near_entry(2 * j + i, o) for o in range(4)])
+            totals.append(dot_nt(left, right, None))
+        close[:, at] = two(*totals)
+        return carry
+
+    def near_share(step):
+        if step == 2:
+            for copy in edges:
+                copy.wait_recv()
+            cells[0] = halo[0]
+            cells[leaves + 1] = halo[1]
+        pairs = leaves // 2
+        share = -(-pairs // (n_z // 2 - 2))
+        lax.fori_loop(min(pairs, (step - 2) * share), min(pairs, (step - 1) * share), near_pair, 0)
+
     select(0)
     for step in range(1, n_z // 2 + 1):
         for way, part in order:
@@ -186,104 +277,68 @@
         select(step)
         if step < n_z // 2:
             select(n_z - step)
-    for copy in arriving + edges:
+        if step >= 2:
+            near_share(step)
+    for copy in arriving:
         copy.wait_recv()
     for copy in sent:
         copy.wait_send()
 
 
-def fetch(samples, points, requests, n_leaf):
+def fetch(samples, points, table, n_leaf):
     n_z = n_leaf // ROWS_Y
     rows = samples.shape[0]
-    half, cell = requests // HALF, requests % HALF
-    places = jnp.stack([half * (SUB // CELL) + cell, half * SUB + HALF * CELL + cell * 2])
-    sent_requests = jnp.swapaxes(places.reshape(2, ROWS_Y, n_z * CAP), 0, 1)
-    sent_requests = jnp.pad(sent_requests, ((0, 0), (0, 6), (0, 0)))
+    leaves = samples.shape[1] // LEAF
     dma = pltpu.SemaphoreType.DMA
     f32 = jnp.float32
     return pl.pallas_call(
         functools.partial(fetch_body, n_leaf),
         out_shape=(
             jax.ShapeDtypeStruct((n_leaf, MSG, 2 * LEAF), f32),
-            jax.ShapeDtypeStruct((2 * SUB, 2 * LEAF), f32),
-            jax.ShapeDtypeStruct((2, NODE, 2 * LEAF), f32),
+            jax.ShapeDtypeStruct(samples.shape, f32),
         ),
-        in_specs=[whole, whole, whole],
-        out_specs=(whole, whole, whole),
-        scratch_shapes=[VMEM((2 * SUB, 2 * LEAF), f32)] * (n_z - 1)
+        in_specs=[whole] * 3,
+        out_specs=(whole, whole),
+        scratch_shapes=[VMEM((2 * SUB, 2 * LEAF), f32)] * n_z
         + [
+            pltpu.SMEM(table.shape, jnp.int32),
+            VMEM((leaves + 2, NODE, 2 * LEAF), f32),
+            VMEM((2, NODE, 2 * LEAF), f32),
             VMEM((ROWS_Y - 1, n_z, MSG, 2 * LEAF), f32),
             VMEM((2, NODE, 2 * LEAF), f32),
-            VMEM((ROWS_Y - 1, 8, n_z * CAP), jnp.int32),
-            pltpu.SMEM((ROWS_Y, 8, n_z * CAP), jnp.int32),
+            VMEM((ROWS_Y - 1, CAP, table.shape[1]), jnp.int32),
+            pltpu.SMEM((ROWS_Y - 1, CAP, table.shape[1]), jnp.int32),
             dma((2, 2, n_z // 2)),
             dma((2, 2, n_z // 2)),
             dma((ROWS_Y - 1, n_z)),
             dma((ROWS_Y - 1, n_z)),
             dma((ROWS_Y - 1,)),
             dma((ROWS_Y - 1,)),
+            dma,
             dma((2,)),
             dma((2,)),
-            dma((2,)),
+            dma,
         ],
         compiler_params=pltpu.CompilerParams(
             collective_id=1, has_side_effects=True, vmem_limit_bytes=40 * MIB
         ),
         name="fetch",
-    )(samples, points, sent_requests)
+    )(samples, points, table)
 
 
 def sample_body(
-    leaves, n_leaf, recv, local, halo, points, slots, counts, near, sketch, far_out, near_out, partial_out, cells
+    leaves, n_leaf, recv, near_in, points, table, sketch, far_out, near_out, partial_out, far_again, scalars, sem
 ):
+    move = pltpu.make_async_copy(table, scalars, sem)
+    move.start()
+    near_out[...] = near_in[...]
     n_z = n_leaf // ROWS_Y
     me = lax.axis_index("leaf")
     y, z = me // n_z, me % n_z
-    low16 = lanes((CELL, 2 * LEAF)) < LEAF
-    low1 = lanes((1, 2 * LEAF)) < LEAF
-    low32 = lanes((2 * CELL, 2 * LEAF)) < LEAF
-    for c in range(leaves):
-        base = (c // HALF) * SUB + (c % HALF) * CELL
-        cbase = (c // HALF) * SUB + HALF * CELL + (c % HALF) * 2
-        cells[c + 1, 0:CELL, :] = local[base : base + CELL, :]
-        cells[c + 1, CELL : CELL + 2, :] = local[cbase : cbase + 2, :]
-    cells[0] = halo[0]
-    cells[leaves + 1] = halo[1]
-
-    def halves(value):
-        high = value.astype(jnp.bfloat16)
-        return high, (value - high.astype(jnp.float32)).astype(jnp.bfloat16)
-
-    def pair(coordinates, first, second):
-        (block_a, row_a, last_a, scale_a), (block_b, row_b, last_b, scale_b) = first, second
-        x = jnp.where(low1, row_a, swap_halves(row_b))
-        yy = jnp.where(low1, swap_halves(row_a), row_b)
-        zz = jnp.where(low1, last_a, last_b)
-        dx = coordinates[0] - x
-        dy = coordinates[1] - yy
-        dz = coordinates[2] - zz
-        square = dx * dx + dy * dy + dz * dz
-        values = jnp.exp2(square * lax.rsqrt(jnp.maximum(square, 1e-30)) * (-1.4426950408889634 / length_scale))
-        block_a = block_a * scale_a
-        block_b = block_b * scale_b
-        rows = jnp.concatenate(
-            [jnp.where(low16, block_a, swap_halves(block_b)), jnp.where(low16, swap_halves(block_a), block_b)], axis=0
-        )
-        return halves(values), halves(rows)
-
-    def four(coordinates, entries):
-        (k0h, k0l), (s0h, s0l) = pair(coordinates, entries[0], entries[1])
-        (k1h, k1l), (s1h, s1l) = pair(coordinates, entries[2], entries[3])
-        left = jnp.concatenate(
-            [jnp.concatenate([s0h, s1h], axis=1), jnp.concatenate([s0l, s1l], axis=1)], axis=0
-        )
-        right = jnp.concatenate(
-            [jnp.concatenate([k0h, k1h], axis=1), jnp.concatenate([k0l, k1l], axis=1)], axis=0
-        )
-        return left, right
+    move.wait()
 
     def far_entry(leaf, f, count):
-        slot = slots[f, leaf]
+        slot = scalars[SLOT_ROW + f, leaf]
         owner = slot >> 3
         message = ((y - owner // n_z) & (ROWS_Y - 1)) * n_z + ((z - owner) & (n_z - 1))
         c = slot & (CAP - 1)
@@ -295,29 +350,11 @@
             scale,
         )
 
-    def near_entry(leaf, offset):
-        at = leaf + offset
-        if offset < NEAR:
-            place = me * leaves + leaf + offset - NEAR // 2
-            inside = (place >= 0) & (place < n_leaf * leaves)
-            scale = jnp.where(inside, near[offset, leaf], 0).astype(jnp.float32)
-        else:
-            scale = jnp.float32(0)
-        at = at if offset < NEAR else leaf
-        return cells[at, 0:CELL, :], cells[at, CELL : CELL + 1, :], cells[at, CELL + 1 : CELL + 2, :], scale
-
-    def fold(total):
-        total = total[: 2 * CELL] + total[2 * CELL :]
-        return total + swap_halves(total)
-
     def two_leaves(j, carry):
         pair_of = (2 * j, 2 * j + 1)
-        coordinates = []
-        both = points[:, pl.ds(pl.multiple_of(j * 2 * LEAF, 2 * LEAF), 2 * LEAF)]
-        both = jnp.concatenate([both, jnp.zeros((5, 2 * LEAF), jnp.float32)], axis=0).T
-        for block in (both[:LEAF], both[LEAF:]):
-            coordinates.append([jnp.broadcast_to(block[:, a : a + 1], (LEAF, 2 * LEAF)) for a in range(3)])
-        count = [counts[leaf] for leaf in pair_of]
+        at = pl.ds(pl.multiple_of(j * 2 * LEAF, 2 * LEAF), 2 * LEAF)
+        coordinates = columns_of(points[:, at])
+        count = [scalars[COUNT_ROW, leaf] for leaf in pair_of]
 
         def operands(g):
             return [
@@ -333,30 +370,30 @@
         steps = (jnp.maximum(count[0], count[1]) + 3) // 4
         totals, waiting = lax.fori_loop(1, steps, step, ([zero, zero], operands(0)))
         far = [total + dot_nt(left, right, None) for total, (left, right) in zip(totals, waiting)]
-        close = [four(coordinates[i], [near_entry(pair_of[i], o) for o in range(4)]) for i in range(2)]
-        close = [dot_nt(left, right, None) for left, right in close]
-        far = jnp.where(low32, fold(far[0]), fold(far[1]))
-        at = pl.ds(pl.multiple_of(j * 2 * LEAF, 2 * LEAF), 2 * LEAF)
+        far = two(*far)
         far_out[:, at] = far
-        near_out[:, at] = jnp.where(low32, fold(close[0]), fold(close[1]))
+        far_again[:, at] = far
         partial_out[:, at] = dot_nn(sketch[...], far)
         return carry
 
     lax.fori_loop(0, leaves // 2, two_leaves, 0)
 
 
-def sample(recv, local, halo, points, slots, counts, near, sketch, n_leaf):
-    leaves = counts.shape[0]
+def sample(recv, near, points, table, sketch, n_leaf):
+    leaves = points.shape[1] // LEAF
     shape = jax.ShapeDtypeStruct((RANK, leaves * LEAF), jnp.float32)
     return pl.pallas_call(
         functools.partial(sample_body, leaves, n_leaf),
-        out_shape=(shape, shape, shape),
-        in_specs=[whole, whole, whole, whole, scalars, scalars, scalars, whole],
-        out_specs=(whole, whole, whole),
-        scratch_shapes=[VMEM((leaves + 2, NODE, 2 * LEAF), jnp.float32)],
+        out_shape=(shape, shape, shape, shape),
+        in_specs=[whole] * 5,
+        out_specs=(whole, whole, whole, whole),
+        scratch_shapes=[
+            pltpu.SMEM(table.shape, jnp.int32),
+            pltpu.SemaphoreType.DMA,
+        ],
         compiler_params=pltpu.CompilerParams(vmem_limit_bytes=40 * MIB),
         name="sample",
-    )(recv, local, halo, points, slots, counts, near, sketch)
+    )(recv, near, points, table, sketch)
 
 
 def eye(shape, first=0):
@@ -366,7 +403,6 @@
 
 def inverse(value):
     guess = pl.reciprocal(value, approx=True)
-    guess = guess * (2.0 - value * guess)
     return guess * (2.0 - value * guess)
 
 
@@ -393,28 +429,23 @@
                 pivot = jnp.broadcast_to(column[0][t][s : s + 1], full)
                 inv = inverse(pivot)
                 scale[g] = jnp.where(sub == s, lax.rsqrt(pivot), scale[g])
-                row = jnp.broadcast_to(tile[g][s : s + 1], full) * inv
+                row = jnp.broadcast_to(tile[g][s : s + 1], full)
                 right = [None] * block
                 for u in range(t + 1, block):
-                    right[u] = jnp.broadcast_to(column[0][u][s : s + 1], full) * inv
+                    right[u] = jnp.broadcast_to(column[0][u][s : s + 1], full)
                 for h in range(g, 4):
                     c = column[h - g][t]
                     if h == g:
                         if s == 7:
                             continue
                         c = jnp.where(sub > s, c, 0.0)
-                    tile[h] = tile[h] - c * row
+                    tile[h] = tile[h] - (c * row) * inv
                     for u in range(t + 1, block):
-                        column[h - g][u] = column[h - g][u] - c * right[u]
+                        column[h - g][u] = column[h - g][u] - (c * right[u]) * inv
     return [
         jnp.concatenate([part * factor for part, factor in zip(tile, scale)], axis=0)
         for tile, scale in zip(tiles, scales)
     ]
-
-
-def halves(value):
-    high = value.astype(jnp.bfloat16)
-    return high, (value - high.astype(jnp.float32)).astype(jnp.bfloat16)
 
 
 def total_of(value):
@@ -791,12 +822,17 @@
 
 
 def on_device(n_leaf, n_cols, points, samples, sketch, far_requests, far_slots, far_count, near_mask):
-    recv, local, halo = fetch(samples, points, far_requests[0], n_leaf)
-    far_sample, near_sample, partial = sample(
-        recv, local, halo, points, far_slots.T, far_count, near_mask.T, sketch, n_leaf
+    table = jnp.concatenate(
+        [
+            jnp.pad(rows, ((0, 0), (0, 2 * LEAF - rows.shape[1])))
+            for rows in (far_requests[0].T, far_slots.T, near_mask.T, far_count[None], jnp.zeros((4, LEAF), jnp.int32))
+        ],
+        axis=0,
     )
+    recv, close = fetch(samples, points, table, n_leaf)
+    far_sample, near_sample, partial, far_again = sample(recv, close, points, table, sketch, n_leaf)
     tiles = leaf_tiles(partial, n_cols)
-    leaf_basis, branch_samples, top_transfer, root_sample = tree(tiles, far_sample, n_leaf, n_cols)
+    leaf_basis, branch_samples, top_transfer, root_sample = tree(tiles, far_again, n_leaf, n_cols)
     return far_sample, near_sample, leaf_basis, branch_samples, jnp.swapaxes(top_transfer, 1, 2), root_sample
 
 

time: 161 us -> 157 us (0.975)
  Pallas kernels: 150 us -> 148 us
    pallas_call x1, Pallas kernels: 17.7 us -> 12.4 us  [sample(): pl.pallas_call(functools.partial(sample_body, leaves, n_leaf), out_shape=...]
    pallas_call x1, Pallas kernels: 38 us -> 41.3 us  [tree(): pl.pallas_call(functools.partial(tree_body, n_leaf, n_cols), out_shape=(j...]
    unnamed x18 -> x10, local copies, waits for them, and re-layouts: 8.27 us -> 5.29 us
    pad x1 -> x6, local copies, waits for them, and re-layouts: 0.01 us -> 2.75 us  [on_device(): jnp.pad(rows, ((0, 0), (0, 2 * LEAF - rows.shape[1])))]
where the time goes in v2:
time: 157 us; the launch traced here: 156 us
  Pallas kernels  148 us (94%)
  local copies, waits for them, and re-layouts  8.07 us (5%)
    pallas_call x1, Pallas kernels, fetch(): pl.pallas_call(functools.partial(fetch_body, n_leaf), out_shape=(jax.Shap...  69.1 us
    pallas_call x1, Pallas kernels, tree(): pl.pallas_call(functools.partial(tree_body, n_leaf, n_cols), out_shape=(j...  41.3 us
    pallas_call x1, Pallas kernels, leaf_tiles(): pl.pallas_call(functools.partial(leaf_body, n_cols), out_shape=jax.ShapeD...  24.9 us
    pallas_call x1, Pallas kernels, sample(): pl.pallas_call(functools.partial(sample_body, leaves, n_leaf), out_shape=...  12.4 us
    unnamed x10, local copies, waits for them, and re-layouts  5.29 us

profile of v2, /device:TPU:1, one launch (start us, length us, event | category | flops | bytes accessed | tf_op | source)
XLA Modules:
  0.0 156.4 jit_solution(17953898453889365784)
XLA Ops:
  0.6 0.7 pad.25
  1.3 0.7 pad.24
  2.0 0.7 pad.22
  2.7 0.7 pad.23
  3.4 0.0 copy-start
  3.4 0.9 copy-done
  4.4 0.0 copy-start.1
  4.4 0.8 copy-done.1
  5.1 69.1 %fetch.1 = (f32[64,144,128]{2,1,0:T(8,128)S(1)}, f32[32,2048]{1,0:T(8,128)S(1)}) custom-call(f32[32,2048]{1,0:T(8,128)S(1)} %copy-done, f32[3,2048]{1,0:T(4,128)S(1)} %copy-done.1, s32[32,128]{1,0:T(8,128)S(1)} %concatenate.3.table), custom_call_target="tpu_custom_call" | custom-call | tf_op jit(solution)/shard_map/fetch/pallas_call | solution.py:294
  74.2 0.0 copy-start.2
  74.2 0.7 copy-done.2
  74.9 12.4 %sample.1 = (f32[32,2048]{1,0:T(8,128)}, f32[32,2048]{1,0:T(8,128)}, f32[32,2048]{1,0:T(8,128)S(1)}, f32[32,2048]{1,0:T(8,128)S(1)}) custom-call(f32[64,144,128]{2,1,0:T(8,128)S(1)} %get-tuple-element.16.recv, f32[32,2048]{1,0:T(8,128)S(1)} %get-tuple-element.17.near_in, f32[3,2048]{1,0:T(4,128)S(1)} %copy-done.1, s32[32,128]{1,0:T(8,128)S(1)} %concatenate.3.table, ...), custom_call_target="tpu_custom_call" | custom-call | tf_op jit(solution)/shard_map/sample/pallas_call | solution.py:385
  87.3 24.9 %leaf_tiles.1.tiles = f32[8,4,32,128]{3,2,1,0:T(8,128)S(1)} custom-call(f32[32,2048]{1,0:T(8,128)S(1)} %get-tuple-element.20.partial), custom_call_target="tpu_custom_call" | custom-call | tf_op jit(solution)/shard_map/leaf_tiles/pallas_call | solution.py:580
  112.3 41.3 %tree.1 = (f32[32,2048]{1,0:T(8,128)S(1)}, f32[32,32]{1,0:T(8,128)S(1)}, f32[63,32,64]{2,1,0:T(8,128)S(1)}, f32[32,32]{1,0:T(8,128)S(1)}) custom-call(f32[8,4,32,128]{3,2,1,0:T(8,128)S(1)} %leaf_tiles.1.tiles, f32[32,2048]{1,0:T(8,128)S(1)} %get-tuple-element.21.far), custom_call_target="tpu_custom_call" | custom-call | tf_op jit(solution)/shard_map/tree/pallas_call | solution.py:788
  153.5 0.7 copy.17
  154.3 0.6 copy.18
  154.9 1.0 copy.19
  155.8 0.6 copy.20
  (4 shorter events, 0.0 us)
Async XLA Ops:
  3.4 0.9 copy-start
  4.4 0.8 copy-start.1
  74.2 0.7 copy-start.2

commit v3 on v2

--- a/solution.py
+++ b/solution.py
@@ -108,7 +108,7 @@
 
 
 def fetch_body(
-    n_leaf, samples, points, table, recv, close, *scratch
+    n_leaf, samples, points, table, recv, close, columns, *scratch
 ):
     n_y = ROWS_Y
     n_z = n_leaf // n_y
@@ -251,6 +251,9 @@
     def near_pair(j, carry):
         at = pl.ds(pl.multiple_of(j * 2 * LEAF, 2 * LEAF), 2 * LEAF)
         coordinates = columns_of(points[:, at])
+        for i in range(2):
+            for a in range(3):
+                columns[2 * j + i, a] = coordinates[i][a]
         totals = []
         for i in range(2):
             left, right = four(coordinates[i], [near_entry(2 * j + i, o) for o in range(4)])
@@ -296,9 +299,10 @@
         out_shape=(
             jax.ShapeDtypeStruct((n_leaf, MSG, 2 * LEAF), f32),
             jax.ShapeDtypeStruct(samples.shape, f32),
+            jax.ShapeDtypeStruct((leaves, 3, LEAF, 2 * LEAF), f32),
         ),
         in_specs=[whole] * 3,
-        out_specs=(whole, whole),
+        out_specs=(whole, whole, whole),
         scratch_shapes=[VMEM((2 * SUB, 2 * LEAF), f32)] * n_z
         + [
             pltpu.SMEM(table.shape, jnp.int32),
@@ -327,11 +331,12 @@
 
 
 def sample_body(
-    leaves, n_leaf, recv, near_in, points, table, sketch, far_out, near_out, partial_out, far_again, scalars, sem
+    leaves, n_leaf, recv, near_in, columns, table, sketch, far_out, near_out, partial_out, far_again, totals, scalars, sem
 ):
     move = pltpu.make_async_copy(table, scalars, sem)
     move.start()
     near_out[...] = near_in[...]
+    totals[...] = jnp.zeros(totals.shape, jnp.float32)
     n_z = n_leaf // ROWS_Y
     me = lax.axis_index("leaf")
     y, z = me // n_z, me % n_z
@@ -350,37 +355,46 @@
             scale,
         )
 
-    def two_leaves(j, carry):
-        pair_of = (2 * j, 2 * j + 1)
-        at = pl.ds(pl.multiple_of(j * 2 * LEAF, 2 * LEAF), 2 * LEAF)
-        coordinates = columns_of(points[:, at])
-        count = [scalars[COUNT_ROW, leaf] for leaf in pair_of]
-
-        def operands(g):
-            return [
-                four(coordinates[i], [far_entry(pair_of[i], 4 * g + b, count[i]) for b in range(4)]) for i in range(2)
-            ]
-
-        def step(g, carried):
-            totals, waiting = carried
-            totals = [total + dot_nt(left, right, None) for total, (left, right) in zip(totals, waiting)]
-            return totals, operands(g)
-
-        zero = jnp.zeros((LEAF, 2 * LEAF), jnp.float32)
-        steps = (jnp.maximum(count[0], count[1]) + 3) // 4
-        totals, waiting = lax.fori_loop(1, steps, step, ([zero, zero], operands(0)))
-        far = [total + dot_nt(left, right, None) for total, (left, right) in zip(totals, waiting)]
-        far = two(*far)
+    def steps_of(leaf):
+        return (scalars[COUNT_ROW, leaf] + 3) // 4
+
+    def operands(leaf, g):
+        count = scalars[COUNT_ROW, leaf]
+        place = jnp.minimum(leaf, leaves - 1)
+        coordinates = [columns[place, a] for a in range(3)]
+        return four(coordinates, [far_entry(leaf, 4 * g + b, count) for b in range(4)])
+
+    def following(leaf, g):
+        last = g + 1 >= steps_of(leaf)
+        return jnp.where(last, jnp.minimum(leaf + 1, leaves), leaf), jnp.where(last, 0, g + 1)
+
+    def work(leaf, g):
+        second = following(leaf, g)
+        return following(*second), (leaf, second[0]), (operands(leaf, g), operands(*second))
+
+    def add(places, waiting):
+        for place, (left, right) in zip(places, waiting):
+            totals[place] += dot_nt(left, right, None)
+
+    def turn(t, carried):
+        at, places, waiting = carried
+        add(places, waiting)
+        return work(*at)
+
+    zero = jnp.int32(0)
+    steps = lax.fori_loop(0, leaves, lambda leaf, total: total + steps_of(leaf), zero)
+    at, places, waiting = lax.fori_loop(1, (steps + 1) // 2, turn, work(zero, zero))
+    add(places, waiting)
+    for j in range(leaves // 2):
+        at = pl.ds(j * 2 * LEAF, 2 * LEAF)
+        far = two(totals[2 * j], totals[2 * j + 1])
         far_out[:, at] = far
         far_again[:, at] = far
         partial_out[:, at] = dot_nn(sketch[...], far)
-        return carry
-
-    lax.fori_loop(0, leaves // 2, two_leaves, 0)
-
-
-def sample(recv, near, points, table, sketch, n_leaf):
-    leaves = points.shape[1] // LEAF
+
+
+def sample(recv, near, columns, table, sketch, n_leaf):
+    leaves = columns.shape[0]
     shape = jax.ShapeDtypeStruct((RANK, leaves * LEAF), jnp.float32)
     return pl.pallas_call(
         functools.partial(sample_body, leaves, n_leaf),
@@ -388,12 +402,13 @@
         in_specs=[whole] * 5,
         out_specs=(whole, whole, whole, whole),
         scratch_shapes=[
+            VMEM((leaves + 1, LEAF, 2 * LEAF), jnp.float32),
             pltpu.SMEM(table.shape, jnp.int32),
             pltpu.SemaphoreType.DMA,
         ],
         compiler_params=pltpu.CompilerParams(vmem_limit_bytes=40 * MIB),
         name="sample",
-    )(recv, near, points, table, sketch)
+    )(recv, near, columns, table, sketch)
 
 
 def eye(shape, first=0):
@@ -632,7 +647,7 @@
 
 def tree_body(
     n_leaf, n_cols, tiles, far, basis, branch, transfers, root,
-    upper, samples, top_samples, chosen, packed_p, out_p,
+    upper, chosen, packed_p, out_p,
     yc_send, yc_recv, zc_send, zc_recv, yp_send, yp_recv, zp_send, zp_recv, x_send, x_recv, own,
 ):
     n_y = ROWS_Y
@@ -652,6 +667,17 @@
 
     levels = chain([tiles[c, 3] for c in range(n_cols)])
     packed_c = pack(levels[-1][0], RANK)
+
+    values = []
+    for c in range(n_cols):
+        leaves = []
+        for j in range(2):
+            at = pl.ds((2 * c + j) * 2 * LEAF, 2 * LEAF)
+            pair, rows = tiles[c, j], far[:, at]
+            basis[:, at] = pair
+            leaves += [project_t(q, row) for q, row in zip(both(pair), both(rows))]
+        values.append(leaves)
+    values = [climb(tiles, c, leaves) for c, leaves in enumerate(values)]
     pl.semaphore_wait(barrier, len(across) + len(along) + len(others))
 
     tree_y, tree_z = (col * seg) // n_z, (col * seg) % n_z
@@ -671,23 +697,7 @@
         for k in range(n_y - 1):
             c_across(k).start()
 
-    def lower(g, carry):
-        owners = [4 * g + b for b in range(4)]
-        values = []
-        for c in owners:
-            leaves = []
-            for j in range(2):
-                at = pl.ds(pl.multiple_of((2 * c + j) * 2 * LEAF, 2 * LEAF), 2 * LEAF)
-                pair, rows = tiles[c, j], far[:, at]
-                basis[:, at] = pair
-                leaves += [project_t(q, row) for q, row in zip(both(pair), both(rows))]
-            values.append(leaves)
-        for c, leaves in zip(owners, values):
-            samples[c] = climb(tiles, c, leaves)
-        return carry
-
-    lax.fori_loop(0, n_cols // 4, lower, 0)
-    value = finish(levels, [samples[c] for c in range(n_cols)])
+    value = finish(levels, values)
     branch[...] = value
     packed_p[...] = pack(jnp.concatenate([value, jnp.zeros((RANK, 3 * RANK), jnp.float32)], axis=1), 0)
 
@@ -728,43 +738,36 @@
         parent_tile(jnp.concatenate([unpack(chosen[2 * i]), unpack(chosen[2 * i + 1])], axis=0)) for i in range(seg // 2)
     ]
     collect, end = subtree(n_cols, [tile for tile, _ in pairs], [trace for _, trace in pairs], upper, x_send, x_recv)
-    collect(2)
-    levels = chain([upper[c, 3] for c in range(n_cols)])
-    collect(0)
-    collect(1)
+    for part in (0, 1, 2):
+        collect(part)
     for k in range(n_z - 1):
         other = (z + n_z - k - 1) % n_z
         descriptor(out_p.at[other], out_p.at[other], zp_send.at[k], zp_recv.at[k], "leaf", along[k]).wait_recv()
 
     def q_of(tile):
-        return tile[:, : 2 * RANK]
-
-    def higher(g, carry):
-        owners = [4 * g + b for b in range(4)]
-        values = []
-        for c in owners:
-            nodes = []
-            for j in range(2):
-                for i, tile in enumerate(both(upper[c, j])):
-                    at = c * seg + 2 * (2 * j + i)
-                    children = [unpack(out_p[(at + d) % n_z, (at + d) // n_z]) for d in range(2)]
-                    nodes.append(project(tile, jnp.concatenate(children, axis=0)))
-                    transfers[4 * c + 2 * j + i] = q_of(swap_halves(tile))
-            values.append(nodes)
-        for c, nodes in zip(owners, values):
-            for i, tile in enumerate(both(upper[c, 2])):
-                transfers[4 * n_cols + 2 * c + i] = q_of(swap_halves(tile))
-            transfers[6 * n_cols + c] = q_of(swap_halves(upper[c, 3]))
-            top_samples[c] = climb(upper, c, nodes)
-        return carry
-
-    lax.fori_loop(0, n_cols // 4, higher, 0)
+        return swap_halves(tile)[:, : 2 * RANK]
+
+    levels = chain([upper[c, 3] for c in range(n_cols)])
+    values = []
+    for c in range(n_cols):
+        nodes = []
+        for j in range(2):
+            for i, tile in enumerate(both(upper[c, j])):
+                at = c * seg + 2 * (2 * j + i)
+                children = [unpack(out_p[(at + d) % n_z, (at + d) // n_z]) for d in range(2)]
+                nodes.append(project(tile, jnp.concatenate(children, axis=0)))
+                transfers[4 * c + 2 * j + i] = q_of(tile)
+        values.append(nodes)
+        for i, tile in enumerate(both(upper[c, 2])):
+            transfers[4 * n_cols + 2 * c + i] = q_of(tile)
+        transfers[6 * n_cols + c] = q_of(upper[c, 3])
+    values = [climb(upper, c, nodes) for c, nodes in enumerate(values)]
     first = 7 * n_cols
     for level_tiles in levels:
         for i, tile in enumerate(level_tiles):
-            transfers[first + i] = q_of(swap_halves(tile))
+            transfers[first + i] = q_of(tile)
         first += len(level_tiles)
-    root[...] = finish(levels, [top_samples[c] for c in range(n_cols)])[:, :RANK]
+    root[...] = finish(levels, values)[:, :RANK]
 
     @pl.when(starts)
     def _():
@@ -797,8 +800,6 @@
         out_specs=(whole, whole, whole, whole),
         scratch_shapes=[
             VMEM((n_cols, 4, RANK, 4 * RANK), f32),
-            VMEM((n_cols, RANK, RANK), f32),
-            VMEM((n_cols, RANK, 4 * RANK), f32),
             VMEM((n_leaf // n_cols, 8, 4 * RANK), f32),
             VMEM((8, 4 * RANK), f32),
             VMEM((n_z, ROWS_Y, 8, 4 * RANK), f32),
@@ -822,15 +823,11 @@
 
 
 def on_device(n_leaf, n_cols, points, samples, sketch, far_requests, far_slots, far_count, near_mask):
-    table = jnp.concatenate(
-        [
-            jnp.pad(rows, ((0, 0), (0, 2 * LEAF - rows.shape[1])))
-            for rows in (far_requests[0].T, far_slots.T, near_mask.T, far_count[None], jnp.zeros((4, LEAF), jnp.int32))
-        ],
-        axis=0,
-    )
-    recv, close = fetch(samples, points, table, n_leaf)
-    far_sample, near_sample, partial, far_again = sample(recv, close, points, table, sketch, n_leaf)
+    table = jnp.zeros((32, 2 * LEAF), jnp.int32)
+    for row, block in ((0, far_requests[0].T), (SLOT_ROW, far_slots.T), (MASK_ROW, near_mask.T), (COUNT_ROW, far_count[None])):
+        table += jnp.pad(block, ((row, 32 - row - block.shape[0]), (0, 2 * LEAF - block.shape[1])))
+    recv, close, columns = fetch(samples, points, table, n_leaf)
+    far_sample, near_sample, partial, far_again = sample(recv, close, columns, table, sketch, n_leaf)
     tiles = leaf_tiles(partial, n_cols)
     leaf_basis, branch_samples, top_transfer, root_sample = tree(tiles, far_again, n_leaf, n_cols)
     return far_sample, near_sample, leaf_basis, branch_samples, jnp.swapaxes(top_transfer, 1, 2), root_sample

time: 157 us -> 147 us (0.936)
  Pallas kernels: 148 us -> 140 us
  local copies, waits for them, and re-layouts: 8.07 us -> 5.29 us
    pallas_call x1, Pallas kernels: 41.3 us -> 34.8 us  [tree(): pl.pallas_call(functools.partial(tree_body, n_leaf, n_cols), out_shape=(j...]
    pad x6 -> x0, local copies, waits for them, and re-layouts: 2.75 us -> none  [on_device(): jnp.pad(rows, ((0, 0), (0, 2 * LEAF - rows.shape[1])))]
where the time goes in v3:
time: 147 us
  Pallas kernels  140 us (95%)
  local copies, waits for them, and re-layouts  5.29 us (4%)
    pallas_call x1, Pallas kernels, fetch(): pl.pallas_call(functools.partial(fetch_body, n_leaf), out_shape=(jax.Shap...  69.1 us
    pallas_call x1, Pallas kernels, tree(): pl.pallas_call(functools.partial(tree_body, n_leaf, n_cols), out_shape=(j...  34.8 us
    pallas_call x1, Pallas kernels, leaf_tiles(): pl.pallas_call(functools.partial(leaf_body, n_cols), out_shape=jax.ShapeD...  24.9 us
    pallas_call x1, Pallas kernels, sample(): pl.pallas_call(functools.partial(sample_body, leaves, n_leaf), out_shape=...  11.3 us
    unnamed x10, local copies, waits for them, and re-layouts  5.29 us

profile of v3, /device:TPU:1, one launch (start us, length us, event | category | flops | bytes accessed | tf_op | source)
XLA Modules:
  0.0 146.7 jit_solution(14171161546539885829)
XLA Ops:
  0.6 0.7 pad_add_fusion.table
  1.4 0.0 copy-start
  1.4 0.9 copy-done
  2.3 0.0 copy-start.1
  2.3 0.8 copy-done.1
  3.1 69.1 %fetch.1 = (f32[64,144,128]{2,1,0:T(8,128)S(1)}, f32[32,2048]{1,0:T(8,128)S(1)}, f32[32,3,64,128]{3,2,1,0:T(8,128)S(1)}) custom-call(f32[32,2048]{1,0:T(8,128)S(1)} %copy-done, f32[3,2048]{1,0:T(4,128)S(1)} %copy-done.1, s32[32,128]{1,0:T(8,128)S(1)} %pad_add_fusion.table), custom_call_target="tpu_custom_call" | custom-call | tf_op jit(solution)/shard_map/fetch/pallas_call | solution.py:297
  72.1 0.0 copy-start.2
  72.2 0.7 copy-done.2
  72.9 11.3 %sample.1 = (f32[32,2048]{1,0:T(8,128)}, f32[32,2048]{1,0:T(8,128)}, f32[32,2048]{1,0:T(8,128)S(1)}, f32[32,2048]{1,0:T(8,128)S(1)}) custom-call(f32[64,144,128]{2,1,0:T(8,128)S(1)} %get-tuple-element.17.recv, f32[32,2048]{1,0:T(8,128)S(1)} %get-tuple-element.18.near_in, f32[32,3,64,128]{3,2,1,0:T(8,128)S(1)} %get-tuple-element.19.columns, ...), custom_call_target="tpu_custom_call" | custom-call | tf_op jit(solution)/shard_map/sample/pallas_call | solution.py:399
  84.1 24.9 %leaf_tiles.1.tiles = f32[8,4,32,128]{3,2,1,0:T(8,128)S(1)} custom-call(f32[32,2048]{1,0:T(8,128)S(1)} %get-tuple-element.22.partial), custom_call_target="tpu_custom_call" | custom-call | tf_op jit(solution)/shard_map/leaf_tiles/pallas_call | solution.py:595
  109.1 34.8 %tree.1 = (f32[32,2048]{1,0:T(8,128)S(1)}, f32[32,32]{1,0:T(8,128)S(1)}, f32[63,32,64]{2,1,0:T(8,128)S(1)}, f32[32,32]{1,0:T(8,128)S(1)}) custom-call(f32[8,4,32,128]{3,2,1,0:T(8,128)S(1)} %leaf_tiles.1.tiles, f32[32,2048]{1,0:T(8,128)S(1)} %get-tuple-element.23.far), custom_call_target="tpu_custom_call" | custom-call | tf_op jit(solution)/shard_map/tree/pallas_call | solution.py:791
  143.9 0.7 copy.17
  144.6 0.6 copy.18
  145.2 1.0 copy.19
  146.1 0.6 copy.20
Async XLA Ops:
  1.4 0.9 copy-start
  2.3 0.8 copy-start.1
  72.1 0.7 copy-start.2

commit v4 on v3

--- a/solution.py
+++ b/solution.py
@@ -104,7 +104,7 @@
     barrier = pltpu.get_barrier_semaphore()
     for peer in peers:
         pl.semaphore_signal(barrier, inc=1, device_id={axis: peer}, device_id_type=MESH)
-    pl.semaphore_wait(barrier, len(peers))
+    return lambda: pl.semaphore_wait(barrier, len(peers))
 
 
 def fetch_body(
@@ -124,7 +124,7 @@
     leaves = samples.shape[1] // LEAF
     read = pltpu.make_async_copy(table, scalars, start_sem)
     read.start()
-    greet("leaf", [up, down, above, below] + across[1:])
+    greet("leaf", [up, down, above, below] + across[1:])()
     own = table.at[pl.ds(0, CAP)]
 
     def remote(src, dst, send, recv_sem, peer):
@@ -222,7 +222,7 @@
         def requests(k):
             return lambda c: (asked[k - 1, c, y * n_z + source_z] if k else scalars[c, y * n_z + source_z])
 
-        for k in range(1, n_y):
+        for k in sorted(range(1, n_y), key=lambda k: -min(k, n_y - k)):
             pick(chunk, stage.at[k - 1, slot], requests(k))
             copy = remote(
                 stage.at[k - 1, slot], recv.at[k * n_z + slot], y_send.at[k - 1, slot], y_recv.at[k - 1, slot], across[k]
@@ -331,7 +331,7 @@
 
 
 def sample_body(
-    leaves, n_leaf, recv, near_in, columns, table, sketch, far_out, near_out, partial_out, far_again, totals, scalars, sem
+    leaves, n_leaf, recv, near_in, columns, table, far_out, near_out, far_again, totals, scalars, sem
 ):
     move = pltpu.make_async_copy(table, scalars, sem)
     move.start()
@@ -390,17 +390,16 @@
         far = two(totals[2 * j], totals[2 * j + 1])
         far_out[:, at] = far
         far_again[:, at] = far
-        partial_out[:, at] = dot_nn(sketch[...], far)
-
-
-def sample(recv, near, columns, table, sketch, n_leaf):
+
+
+def sample(recv, near, columns, table, n_leaf):
     leaves = columns.shape[0]
     shape = jax.ShapeDtypeStruct((RANK, leaves * LEAF), jnp.float32)
     return pl.pallas_call(
         functools.partial(sample_body, leaves, n_leaf),
-        out_shape=(shape, shape, shape, shape),
-        in_specs=[whole] * 5,
-        out_specs=(whole, whole, whole, whole),
+        out_shape=(shape, shape, shape),
+        in_specs=[whole] * 4,
+        out_specs=(whole, whole, whole),
         scratch_shapes=[
             VMEM((leaves + 1, LEAF, 2 * LEAF), jnp.float32),
             pltpu.SMEM(table.shape, jnp.int32),
@@ -408,7 +407,7 @@
         ],
         compiler_params=pltpu.CompilerParams(vmem_limit_bytes=40 * MIB),
         name="sample",
-    )(recv, near, columns, table, sketch)
+    )(recv, near, columns, table)
 
 
 def eye(shape, first=0):
@@ -418,7 +417,7 @@
 
 def inverse(value):
     guess = pl.reciprocal(value, approx=True)
-    return guess * (2.0 - value * guess)
+    return guess
 
 
 def compress(tiles, traces):
@@ -555,11 +554,15 @@
     return collect, end
 
 
-def leaf_body(n_cols, partial, out, pieces, send_a, recv_a, send_b, recv_b):
+def leaf_body(n_cols, far, sketch, out, partial, pieces, send_a, recv_a, send_b, recv_b):
     me = lax.axis_index("cols")
     width = partial.shape[1] // n_cols
     peers = [(me + k) % n_cols for k in range(1, n_cols)]
-    greet("cols", peers)
+    ready = greet("cols", peers)
+    for j in range(partial.shape[1] // (2 * LEAF)):
+        at = pl.ds(j * 2 * LEAF, 2 * LEAF)
+        partial[:, at] = dot_nn(sketch[...], far[:, at])
+    ready()
 
     def piece(owner):
         return pl.ds(pl.multiple_of(owner * width, width), width)
@@ -589,20 +592,20 @@
     end()
 
 
-def leaf_tiles(partial, n_cols):
-    rows, columns = partial.shape
+def leaf_tiles(far, sketch, n_cols):
+    rows, columns = far.shape
     dma = pltpu.SemaphoreType.DMA
     return pl.pallas_call(
         functools.partial(leaf_body, n_cols),
         out_shape=jax.ShapeDtypeStruct((n_cols, 4, RANK, 4 * RANK), jnp.float32),
-        in_specs=[whole],
+        in_specs=[whole, whole],
         out_specs=whole,
-        scratch_shapes=[VMEM((n_cols - 1, rows, columns // n_cols), jnp.float32)]
+        scratch_shapes=[VMEM(far.shape, jnp.float32), VMEM((n_cols - 1, rows, columns // n_cols), jnp.float32)]
         + [dma((n_cols - 1,))] * 2
         + [dma((3, n_cols - 1))] * 2,
         compiler_params=pltpu.CompilerParams(collective_id=2, has_side_effects=True, vmem_limit_bytes=40 * MIB),
         name="leaf_tiles",
-    )(partial)
+    )(far, sketch)
 
 
 def unpack(block):
@@ -646,7 +649,7 @@
 
 
 def tree_body(
-    n_leaf, n_cols, tiles, far, basis, branch, transfers, root,
+    n_leaf, n_cols, tiles, far, branch, transfers, root,
     upper, chosen, packed_p, out_p,
     yc_send, yc_recv, zc_send, zc_recv, yp_send, yp_recv, zp_send, zp_recv, x_send, x_recv, own,
 ):
@@ -674,7 +677,6 @@
         for j in range(2):
             at = pl.ds((2 * c + j) * 2 * LEAF, 2 * LEAF)
             pair, rows = tiles[c, j], far[:, at]
-            basis[:, at] = pair
             leaves += [project_t(q, row) for q, row in zip(both(pair), both(rows))]
         values.append(leaves)
     values = [climb(tiles, c, leaves) for c, leaves in enumerate(values)]
@@ -791,13 +793,12 @@
     return pl.pallas_call(
         functools.partial(tree_body, n_leaf, n_cols),
         out_shape=(
-            jax.ShapeDtypeStruct(far.shape, f32),
             jax.ShapeDtypeStruct((RANK, RANK), f32),
             jax.ShapeDtypeStruct((n_leaf - 1, RANK, 2 * RANK), f32),
             jax.ShapeDtypeStruct((RANK, RANK), f32),
         ),
         in_specs=[whole, whole],
-        out_specs=(whole, whole, whole, whole),
+        out_specs=(whole, whole, whole),
         scratch_shapes=[
             VMEM((n_cols, 4, RANK, 4 * RANK), f32),
             VMEM((n_leaf // n_cols, 8, 4 * RANK), f32),
@@ -822,14 +823,41 @@
     )(tiles, far)
 
 
+def results_body(tiles, branch, transfers, root, basis_out, branch_out, transfers_out, root_out):
+    for c in range(tiles.shape[0]):
+        for j in range(2):
+            basis_out[:, pl.ds((2 * c + j) * 2 * LEAF, 2 * LEAF)] = tiles[c, j]
+    branch_out[...] = branch[...]
+    transfers_out[...] = transfers[...]
+    root_out[...] = root[...]
+
+
+def results(tiles, branch, transfers, root):
+    f32 = jnp.float32
+    return pl.pallas_call(
+        results_body,
+        out_shape=(
+            jax.ShapeDtypeStruct((RANK, 4 * tiles.shape[0] * LEAF), f32),
+            jax.ShapeDtypeStruct(branch.shape, f32),
+            jax.ShapeDtypeStruct(transfers.shape, f32),
+            jax.ShapeDtypeStruct(root.shape, f32),
+        ),
+        in_specs=[whole] * 4,
+        out_specs=(whole,) * 4,
+        compiler_params=pltpu.CompilerParams(vmem_limit_bytes=40 * MIB),
+        name="results",
+    )(tiles, branch, transfers, root)
+
+
 def on_device(n_leaf, n_cols, points, samples, sketch, far_requests, far_slots, far_count, near_mask):
     table = jnp.zeros((32, 2 * LEAF), jnp.int32)
     for row, block in ((0, far_requests[0].T), (SLOT_ROW, far_slots.T), (MASK_ROW, near_mask.T), (COUNT_ROW, far_count[None])):
         table += jnp.pad(block, ((row, 32 - row - block.shape[0]), (0, 2 * LEAF - block.shape[1])))
     recv, close, columns = fetch(samples, points, table, n_leaf)
-    far_sample, near_sample, partial, far_again = sample(recv, close, columns, table, sketch, n_leaf)
-    tiles = leaf_tiles(partial, n_cols)
-    leaf_basis, branch_samples, top_transfer, root_sample = tree(tiles, far_again, n_leaf, n_cols)
+    far_sample, near_sample, far_again = sample(recv, close, columns, table, n_leaf)
+    tiles = leaf_tiles(far_again, sketch, n_cols)
+    branch_samples, top_transfer, root_sample = tree(tiles, far_again, n_leaf, n_cols)
+    leaf_basis, branch_samples, top_transfer, root_sample = results(tiles, branch_samples, top_transfer, root_sample)
     return far_sample, near_sample, leaf_basis, branch_samples, jnp.swapaxes(top_transfer, 1, 2), root_sample
 
 

time: 147 us -> 143 us (0.973)
  local copies, waits for them, and re-layouts: 5.29 us -> 1.71 us
    pallas_call x1, Pallas kernels: 11.3 us -> 5.99 us  [sample(): pl.pallas_call(functools.partial(sample_body, leaves, n_leaf), out_shape=...]
    pallas_call x1, Pallas kernels: 34.8 us -> 39.1 us  [tree(): pl.pallas_call(functools.partial(tree_body, n_leaf, n_cols), out_shape=(j...]
    unnamed x10 -> x6, local copies, waits for them, and re-layouts: 5.29 us -> 1.71 us
where the time goes in v4:
time: 143 us
  Pallas kernels  140 us (98%)
  local copies, waits for them, and re-layouts  1.71 us (1%)
    pallas_call x1, Pallas kernels, fetch(): pl.pallas_call(functools.partial(fetch_body, n_leaf), out_shape=(jax.Shap...  69.7 us
    pallas_call x1, Pallas kernels, tree(): pl.pallas_call(functools.partial(tree_body, n_leaf, n_cols), out_shape=(j...  39.1 us
    pallas_call x1, Pallas kernels, leaf_tiles(): pl.pallas_call(functools.partial(leaf_body, n_cols), out_shape=jax.ShapeD...  23.8 us
    pallas_call x1, Pallas kernels, sample(): pl.pallas_call(functools.partial(sample_body, leaves, n_leaf), out_shape=...  5.99 us

profile of v4, /device:TPU:1, one launch (start us, length us, event | category | flops | bytes accessed | tf_op | source)
XLA Modules:
  0.0 142.9 jit_solution(11679441261216919898)
XLA Ops:
  0.6 0.0 copy-start.2
  0.6 0.7 pad_add_fusion.table
  1.4 0.0 copy-start
  1.4 0.9 copy-done
  2.3 0.0 copy-start.1
  2.3 0.8 copy-done.1
  3.1 69.7 %fetch.1 = (f32[64,144,128]{2,1,0:T(8,128)S(1)}, f32[32,2048]{1,0:T(8,128)S(1)}, f32[32,3,64,128]{3,2,1,0:T(8,128)S(1)}) custom-call(f32[32,2048]{1,0:T(8,128)S(1)} %copy-done, f32[3,2048]{1,0:T(4,128)S(1)} %copy-done.1, s32[32,128]{1,0:T(8,128)S(1)} %pad_add_fusion.table), custom_call_target="tpu_custom_call" | custom-call | tf_op jit(solution)/shard_map/fetch/pallas_call | solution.py:297
  72.8 6.0 %sample.1 = (f32[32,2048]{1,0:T(8,128)}, f32[32,2048]{1,0:T(8,128)}, f32[32,2048]{1,0:T(8,128)S(1)}) custom-call(f32[64,144,128]{2,1,0:T(8,128)S(1)} %get-tuple-element.19.recv, f32[32,2048]{1,0:T(8,128)S(1)} %get-tuple-element.20.near_in, f32[32,3,64,128]{3,2,1,0:T(8,128)S(1)} %get-tuple-element.21.columns, s32[32,128]{1,0:T(8,128)S(1)} %pad_add_fusion.table), custom_call_target="tpu_custom_call" | custom-call | tf_op jit(solution)/shard_map/sample/pallas_call | solution.py:398
  78.8 0.0 copy-done.2
  78.8 23.8 %leaf_tiles.1.tiles = f32[8,4,32,128]{3,2,1,0:T(8,128)S(1)} custom-call(f32[32,2048]{1,0:T(8,128)S(1)} %get-tuple-element.24.far, f32[32,32]{1,0:T(8,128)S(1)} %copy-done.2), custom_call_target="tpu_custom_call" | custom-call | tf_op jit(solution)/shard_map/leaf_tiles/pallas_call | solution.py:598
  102.6 39.1 %tree.1 = (f32[32,32]{1,0:T(8,128)S(1)}, f32[63,32,64]{2,1,0:T(8,128)S(1)}, f32[32,32]{1,0:T(8,128)S(1)}) custom-call(f32[8,4,32,128]{3,2,1,0:T(8,128)S(1)} %leaf_tiles.1.tiles, f32[32,2048]{1,0:T(8,128)S(1)} %get-tuple-element.24.far), custom_call_target="tpu_custom_call" | custom-call | tf_op jit(solution)/shard_map/tree/pallas_call | solution.py:793
  141.7 1.1 results.1
Async XLA Ops:
  0.6 78.2 %copy-start.2 = (f32[32,32]{1,0:T(8,128)S(1)}, f32[32,32]{1,0:T(8,128)}, u32[]{:S(2)}) copy-start(f32[32,32]{1,0:T(8,128)} %sketch.1) | copy-start | bytes 12292
  1.4 0.9 copy-start
  2.3 0.8 copy-start.1

commit v5 on v4

--- a/solution.py
+++ b/solution.py
@@ -124,7 +124,7 @@
     leaves = samples.shape[1] // LEAF
     read = pltpu.make_async_copy(table, scalars, start_sem)
     read.start()
-    greet("leaf", [up, down, above, below] + across[1:])()
+    ready = greet("leaf", [up, down, above, below] + across[1:])
     own = table.at[pl.ds(0, CAP)]
 
     def remote(src, dst, send, recv_sem, peer):
@@ -132,16 +132,6 @@
             src_ref=src, dst_ref=dst, send_sem=send, recv_sem=recv_sem,
             device_id={"leaf": peer}, device_id_type=MESH,
         )
-
-    sent = []
-    asks = []
-    for k in range(1, n_y):
-        copy = remote(
-            own, asked_v.at[n_y - k - 1], q_send.at[k - 1], q_recv.at[n_y - k - 1], across[k]
-        )
-        copy.start()
-        asks.append(copy)
-    sent += asks
 
     low = lanes((CELL, 2 * LEAF)) < LEAF
     for j in range(HALF):
@@ -159,6 +149,24 @@
         local[base + 2 : base + 3, :] = jnp.where(low1, swap_halves(xs), ys)
         local[base + 3 : base + 4, :] = jnp.where(low1, swap_halves(zs), zs)
 
+    for side, cluster in ((0, 0), (1, 2 * HALF - 1)):
+        base = (cluster // HALF) * SUB + (cluster % HALF) * CELL
+        cbase = (cluster // HALF) * SUB + HALF * CELL + (cluster % HALF) * 2
+        edge[side, 0:CELL, :] = local[base : base + CELL, :]
+        edge[side, CELL : CELL + 2, :] = local[cbase : cbase + 2, :]
+        edge[side, CELL + 2 : NODE, :] = jnp.zeros((NODE - CELL - 2, 2 * LEAF), jnp.float32)
+    ready()
+
+    sent = []
+    asks = []
+    for k in range(1, n_y):
+        copy = remote(
+            own, asked_v.at[n_y - k - 1], q_send.at[k - 1], q_recv.at[n_y - k - 1], across[k]
+        )
+        copy.start()
+        asks.append(copy)
+    sent += asks
+
     hops = {(0, 0): n_z // 2, (0, 1): n_z // 2 - 1, (1, 0): n_z // 2 - 1, (1, 1): n_z // 2}
 
     def ring(way, part, step):
@@ -179,12 +187,6 @@
     for way, part in order:
         forward(way, part, 0)
 
-    for side, cluster in ((0, 0), (1, 2 * HALF - 1)):
-        base = (cluster // HALF) * SUB + (cluster % HALF) * CELL
-        cbase = (cluster // HALF) * SUB + HALF * CELL + (cluster % HALF) * 2
-        edge[side, 0:CELL, :] = local[base : base + CELL, :]
-        edge[side, CELL : CELL + 2, :] = local[cbase : cbase + 2, :]
-        edge[side, CELL + 2 : NODE, :] = jnp.zeros((NODE - CELL - 2, 2 * LEAF), jnp.float32)
     edges = [
         remote(edge.at[0], halo.at[1], e_send.at[0], e_recv.at[1], below),
         remote(edge.at[1], halo.at[0], e_send.at[1], e_recv.at[0], above),

time: 143 us -> 143 us (level)
    pallas_call x1, Pallas kernels: 5.99 us -> 9.63 us  [sample(): pl.pallas_call(functools.partial(sample_body, leaves, n_leaf), out_shape=...]
    pallas_call x1, Pallas kernels: 39.1 us -> 36.1 us  [tree(): pl.pallas_call(functools.partial(tree_body, n_leaf, n_cols), out_shape=(j...]
where the time goes in v5:
time: 143 us; the launch traced here: 144 us
  Pallas kernels  140 us (98%)
  local copies, waits for them, and re-layouts  1.71 us (1%)
    pallas_call x1, Pallas kernels, fetch(): pl.pallas_call(functools.partial(fetch_body, n_leaf), out_shape=(jax.Shap...  69.9 us
    pallas_call x1, Pallas kernels, tree(): pl.pallas_call(functools.partial(tree_body, n_leaf, n_cols), out_shape=(j...  36.1 us
    pallas_call x1, Pallas kernels, leaf_tiles(): pl.pallas_call(functools.partial(leaf_body, n_cols), out_shape=jax.ShapeD...  23.5 us
    pallas_call x1, Pallas kernels, sample(): pl.pallas_call(functools.partial(sample_body, leaves, n_leaf), out_shape=...  9.63 us

profile of v5, /device:TPU:1, one launch (start us, length us, event | category | flops | bytes accessed | tf_op | source)
XLA Modules:
  0.0 143.5 jit_solution(4086406253653062487)
XLA Ops:
  0.6 0.0 copy-start.2
  0.6 0.7 pad_add_fusion.table
  1.4 0.0 copy-start
  1.4 0.9 copy-done
  2.3 0.0 copy-start.1
  2.3 0.8 copy-done.1
  3.1 69.9 %fetch.1 = (f32[64,144,128]{2,1,0:T(8,128)S(1)}, f32[32,2048]{1,0:T(8,128)S(1)}, f32[32,3,64,128]{3,2,1,0:T(8,128)S(1)}) custom-call(f32[32,2048]{1,0:T(8,128)S(1)} %copy-done, f32[3,2048]{1,0:T(4,128)S(1)} %copy-done.1, s32[32,128]{1,0:T(8,128)S(1)} %pad_add_fusion.table), custom_call_target="tpu_custom_call" | custom-call | tf_op jit(solution)/shard_map/fetch/pallas_call | solution.py:299
  73.0 9.6 %sample.1 = (f32[32,2048]{1,0:T(8,128)}, f32[32,2048]{1,0:T(8,128)}, f32[32,2048]{1,0:T(8,128)S(1)}) custom-call(f32[64,144,128]{2,1,0:T(8,128)S(1)} %get-tuple-element.19.recv, f32[32,2048]{1,0:T(8,128)S(1)} %get-tuple-element.20.near_in, f32[32,3,64,128]{3,2,1,0:T(8,128)S(1)} %get-tuple-element.21.columns, s32[32,128]{1,0:T(8,128)S(1)} %pad_add_fusion.table), custom_call_target="tpu_custom_call" | custom-call | tf_op jit(solution)/shard_map/sample/pallas_call | solution.py:400
  82.7 0.0 copy-done.2
  82.7 23.5 %leaf_tiles.1.tiles = f32[8,4,32,128]{3,2,1,0:T(8,128)S(1)} custom-call(f32[32,2048]{1,0:T(8,128)S(1)} %get-tuple-element.24.far, f32[32,32]{1,0:T(8,128)S(1)} %copy-done.2), custom_call_target="tpu_custom_call" | custom-call | tf_op jit(solution)/shard_map/leaf_tiles/pallas_call | solution.py:600
  106.2 36.1 %tree.1 = (f32[32,32]{1,0:T(8,128)S(1)}, f32[63,32,64]{2,1,0:T(8,128)S(1)}, f32[32,32]{1,0:T(8,128)S(1)}) custom-call(f32[8,4,32,128]{3,2,1,0:T(8,128)S(1)} %leaf_tiles.1.tiles, f32[32,2048]{1,0:T(8,128)S(1)} %get-tuple-element.24.far), custom_call_target="tpu_custom_call" | custom-call | tf_op jit(solution)/shard_map/tree/pallas_call | solution.py:795
  142.4 1.1 results.1
Async XLA Ops:
  0.6 82.0 %copy-start.2 = (f32[32,32]{1,0:T(8,128)S(1)}, f32[32,32]{1,0:T(8,128)}, u32[]{:S(2)}) copy-start(f32[32,32]{1,0:T(8,128)} %sketch.1) | copy-start | bytes 12292
  1.4 0.9 copy-start
  2.3 0.8 copy-start.1
